TPU v7x, 32 devices: a whole 2x2x4 slice. The times are simulated.
32 devices in a mesh: dp: 8 (over z, x), tower: 4 (over y, core).
Axes of the slice: x: 2, y: 2, z: 4, core: 2. Of those that a mesh axis runs over, the one named last changes fastest.
Arguments:
- tokens: bfloat16 [4, 16, 512, 768], P('tower', 'dp'), may hold values from -6 to 6
- lengths: int32 [4, 16], P('tower', 'dp'), may hold values from 32 to 512, as said below
- positive: int32 [32], replicated, may hold values from 0 to 31, each once
- w_qkv: bfloat16 [768, 2304], replicated, may hold values from -0.21875 to 0.21875
- q_bias: float32 [768], replicated, may hold values from -3 to 3
- v_bias: float32 [768], replicated, may hold values from -3 to 3
- w_out: bfloat16 [768, 768], replicated, may hold values from -1.75 to 1.75
- out_bias: float32 [768], replicated, may hold values from -2 to 2
- norm1_gain: float32 [768], replicated, may hold values from 0.5 to 1.5
- norm1_bias: float32 [768], replicated, may hold values from -2 to 2
- w_up: bfloat16 [768, 3072], replicated, may hold values from -0.21875 to 0.21875
- up_bias: float32 [3072], replicated, may hold values from -3 to 3
- w_down: bfloat16 [3072, 768], replicated, may hold values from -0.109375 to 0.109375
- down_bias: float32 [768], replicated, may hold values from -2 to 2
- norm2_gain: float32 [768], replicated, may hold values from 0.5 to 1.5
- norm2_bias: float32 [768], replicated, may hold values from -0.5 to 0.5
Outputs:
- loss: float32 [], replicated
- grad_tokens: float32 [4, 16, 512, 768], P('tower', 'dp')
- grad_w_qkv: float32 [768, 2304], replicated
- grad_q_bias: float32 [768], replicated
- grad_v_bias: float32 [768], replicated
- grad_w_out: float32 [768, 768], replicated
- grad_out_bias: float32 [768], replicated
- grad_norm1_gain: float32 [768], replicated
- grad_norm1_bias: float32 [768], replicated
- grad_w_up: float32 [768, 3072], replicated
- grad_up_bias: float32 [3072], replicated
- grad_w_down: float32 [3072, 768], replicated
- grad_down_bias: float32 [768], replicated
- grad_norm2_gain: float32 [768], replicated
- grad_norm2_bias: float32 [768], replicated
Inputs may be any that keep to these rules, and one draw needn't show every extreme that they name: `lengths`: one sequence has length exactly 512. Each passage is the positive of exactly one query.
All inputs are finite; a program needn't handle non-finite values.
Results may differ from a plain program's by a relative error of at most 0.0074.
Values sent between devices are 32-bit elements; how exact they have to be, the bound alone decides.
No kernel may reach another device: no remote copies, remote signals or barrier semaphores. Data moves between devices by JAX's collectives and lax.ppermute only.
A program may use at most 192 MiB of HBM per device.

v0:
```python
from functools import partial

import jax
import jax.numpy as jnp
from jax import lax
from jax.sharding import PartitionSpec as P

HD = 64


SOFTMAX_TEMP = 0.01
NORM_EPS = 1e-06
FULL_PRECISION = lax.Precision.HIGHEST


def layer_norm(value_matrix, gain, shift):
    centre = value_matrix - jnp.mean(value_matrix, axis=-1, keepdims=True)
    spread = jnp.mean(centre * centre, axis=-1, keepdims=True)
    return centre * lax.rsqrt(spread + NORM_EPS) * gain + shift


def unit_rows(value_matrix):
    return value_matrix * lax.rsqrt(
        jnp.sum(value_matrix * value_matrix, axis=-1, keepdims=True) + NORM_EPS
    )


def contrast(pooled, positive):
    width = pooled.shape[-1]
    query_batch = unit_rows(pooled[:2].reshape(-1, width))
    passage_batch = unit_rows(pooled[2:].reshape(-1, width))
    similarity_logits = (
        jnp.dot(query_batch, passage_batch.T, precision=FULL_PRECISION) / SOFTMAX_TEMP
    )
    highest = jnp.max(similarity_logits, axis=1, keepdims=True)
    totals = highest[:, 0] + jnp.log(jnp.sum(jnp.exp(similarity_logits - highest), axis=1))
    picked = jnp.where(
        jnp.arange(similarity_logits.shape[1])[None, :] == positive[:, None], similarity_logits, 0.0
    )
    return jnp.mean(totals - jnp.sum(picked, axis=1))


def masked_scores(query_matrix, key_matrix, valid):
    scores = jnp.einsum(
        "uob,pob->oup", query_matrix, key_matrix, preferred_element_type=jnp.float32
    ) * HD ** (-0.5)
    return jnp.where(valid[None, None, :], scores, -1e30)


def attend(items):
    query_matrix, key_matrix, value_matrix, valid = items
    scores = masked_scores(query_matrix, key_matrix, valid)
    highest = jnp.max(scores, axis=-1, keepdims=True)
    expo = jnp.exp(scores - highest)
    summed = jnp.sum(expo, axis=-1, keepdims=True)
    attention_probabilities = (expo / summed).astype(jnp.bfloat16)
    context_vectors = jnp.einsum(
        "zeb,bzf->ezf", attention_probabilities, value_matrix, preferred_element_type=jnp.float32
    )
    return (context_vectors, (highest + jnp.log(summed))[:, :, 0])


def attend_back(items):
    query_matrix, key_matrix, value_matrix, valid, context_gradient, logsum = items
    scores = masked_scores(query_matrix, key_matrix, valid)
    attention_probabilities = jnp.exp(scores - logsum[:, :, None])
    grad_value = jnp.einsum(
        "zku,kzc->uzc",
        attention_probabilities.astype(jnp.bfloat16),
        context_gradient,
        preferred_element_type=jnp.float32,
    )
    probability_gradient = jnp.einsum(
        "uob,pob->oup", context_gradient, value_matrix, preferred_element_type=jnp.float32
    )
    inner = jnp.sum(attention_probabilities * probability_gradient, axis=-1, keepdims=True)
    score_gradient = (attention_probabilities * (probability_gradient - inner)).astype(jnp.bfloat16)
    grad_query = jnp.einsum(
        "zeb,bzf->ezf", score_gradient, key_matrix, preferred_element_type=jnp.float32
    ) * HD ** (-0.5)
    grad_key = jnp.einsum(
        "zku,kzc->uzc", score_gradient, query_matrix, preferred_element_type=jnp.float32
    ) * HD ** (-0.5)
    return (grad_query, grad_key, grad_value)


def local(
    tokens,
    lengths,
    positive,
    w_qkv,
    q_bias,
    v_bias,
    w_out,
    out_bias,
    norm1_gain,
    norm1_bias,
    w_up,
    up_bias,
    w_down,
    down_bias,
    norm2_gain,
    norm2_bias,
):
    seqs, span, width = (tokens.shape[1], tokens.shape[2], tokens.shape[3])
    heads = width // HD
    total_rows = seqs * span
    flat = tokens.reshape(total_rows, width)
    counts = lengths[0]
    valid = jnp.arange(span)[None, :] < counts[:, None]
    bias = jnp.concatenate([q_bias, jnp.zeros_like(q_bias), v_bias])
    proj = (jnp.dot(flat, w_qkv, preferred_element_type=jnp.float32) + bias).astype(jnp.bfloat16)
    proj = proj.reshape(seqs, span, 3, heads, HD)
    query_matrix, key_matrix, value_matrix = (proj[:, :, 0], proj[:, :, 1], proj[:, :, 2])
    context_vectors, logsum = lax.map(attend, (query_matrix, key_matrix, value_matrix, valid))
    context_vectors = context_vectors.reshape(total_rows, width).astype(jnp.bfloat16)
    attn = jnp.dot(context_vectors, w_out, preferred_element_type=jnp.float32) + out_bias
    resid_one = flat.astype(jnp.float32) + attn
    hidden, norm_one_pull = jax.vjp(layer_norm, resid_one, norm1_gain, norm1_bias)
    hidden_low = hidden.astype(jnp.bfloat16)
    upper = jnp.dot(hidden_low, w_up, preferred_element_type=jnp.float32) + up_bias
    active, gelu_pull = jax.vjp(partial(jax.nn.gelu, approximate=False), upper)
    active = active.astype(jnp.bfloat16)
    down = jnp.dot(active, w_down, preferred_element_type=jnp.float32) + down_bias
    output, norm_two_pull = jax.vjp(layer_norm, hidden + down, norm2_gain, norm2_bias)
    mask = valid.astype(jnp.float32)
    sizes = counts[:, None].astype(jnp.float32)
    pooled = jnp.sum(output.reshape(seqs, span, width) * mask[:, :, None], axis=1) / sizes
    grouped = lax.all_gather(pooled[None], "tower", axis=0, tiled=True)
    everything = lax.all_gather(grouped, "dp", axis=1, tiled=True)
    loss, loss_pull = jax.vjp(partial(contrast, positive=positive), everything)
    grad_all = loss_pull(jnp.ones((), jnp.float32))[0]
    grad_own = lax.dynamic_slice(
        grad_all, (lax.axis_index("tower"), lax.axis_index("dp") * seqs, 0), (1, seqs, width)
    )[0]
    grad_output = (
        jnp.broadcast_to((grad_own / sizes)[:, None, :], (seqs, span, width)) * mask[:, :, None]
    ).reshape(total_rows, width)
    grad_resid_two, grad_norm2_gain, grad_norm2_bias = norm_two_pull(grad_output)
    grad_down = grad_resid_two.astype(jnp.bfloat16)
    grad_w_down = jnp.einsum("tf,td->fd", active, grad_down, preferred_element_type=jnp.float32)
    grad_down_bias = jnp.sum(grad_down.astype(jnp.float32), axis=0)
    grad_active = jnp.einsum("td,fd->tf", grad_down, w_down, preferred_element_type=jnp.float32)
    grad_upper = gelu_pull(grad_active)[0].astype(jnp.bfloat16)
    grad_w_up = jnp.einsum("td,tf->df", hidden_low, grad_upper, preferred_element_type=jnp.float32)
    grad_up_bias = jnp.sum(grad_upper.astype(jnp.float32), axis=0)
    grad_hidden = grad_resid_two + jnp.einsum(
        "tf,df->td", grad_upper, w_up, preferred_element_type=jnp.float32
    )
    grad_resid_one, grad_norm1_gain, grad_norm1_bias = norm_one_pull(grad_hidden)
    grad_attn = grad_resid_one.astype(jnp.bfloat16)
    grad_w_out = jnp.einsum(
        "te,td->ed", context_vectors, grad_attn, preferred_element_type=jnp.float32
    )
    grad_out_bias = jnp.sum(grad_attn.astype(jnp.float32), axis=0)
    context_gradient = jnp.einsum(
        "td,ed->te", grad_attn, w_out, preferred_element_type=jnp.float32
    ).astype(jnp.bfloat16)
    context_gradient = context_gradient.reshape(seqs, span, heads, HD)
    grad_query, grad_key, grad_value = lax.map(
        attend_back, (query_matrix, key_matrix, value_matrix, valid, context_gradient, logsum)
    )
    grad_proj = (
        jnp.stack([grad_query, grad_key, grad_value], axis=2)
        .reshape(total_rows, 3 * width)
        .astype(jnp.bfloat16)
    )
    grad_w_qkv = jnp.einsum("td,te->de", flat, grad_proj, preferred_element_type=jnp.float32)
    proj_sums = jnp.sum(grad_proj.astype(jnp.float32), axis=0)
    grad_q_bias = proj_sums[:width]
    grad_v_bias = proj_sums[2 * width :]
    grad_tokens = grad_resid_one + jnp.einsum(
        "te,de->td", grad_proj, w_qkv, preferred_element_type=jnp.float32
    )
    summed = lax.psum(
        (
            grad_w_qkv,
            grad_q_bias,
            grad_v_bias,
            grad_w_out,
            grad_out_bias,
            grad_norm1_gain,
            grad_norm1_bias,
            grad_w_up,
            grad_up_bias,
            grad_w_down,
            grad_down_bias,
            grad_norm2_gain,
            grad_norm2_bias,
        ),
        ("dp", "tower"),
    )
    return (
        loss,
        grad_tokens.reshape(tokens.shape),
        summed[0],
        summed[1],
        summed[2],
        summed[3],
        summed[4],
        summed[5],
        summed[6],
        summed[7],
        summed[8],
        summed[9],
        summed[10],
        summed[11],
        summed[12],
    )


def solution(mesh):
    in_specs = (
        P("tower", "dp", None, None),
        P("tower", "dp"),
        P(),
        P(),
        P(),
        P(),
        P(),
        P(),
        P(),
        P(),
        P(),
        P(),
        P(),
        P(),
        P(),
        P(),
    )
    out_specs = (
        P(),
        P("tower", "dp", None, None),
        P(),
        P(),
        P(),
        P(),
        P(),
        P(),
        P(),
        P(),
        P(),
        P(),
        P(),
        P(),
        P(),
    )
    return jax.shard_map(local, mesh=mesh, in_specs=in_specs, out_specs=out_specs, check_vma=False)
```

profile of v0, /device:TPU:0, one launch (start us, length us, event | category | flops | bytes accessed | tf_op | source)
XLA Modules:
  0.0 798.2 jit_solution(18137250502357723995)
XLA Ops:
  11.2 7.3 add_convert_fusion.1
  18.5 6.6 copy.81
  25.1 8.8 %reshape.315 = bf16[2,512,3,12,64]{1,0,4,3,2:T(2,128)(2,1)} reshape(bf16[1024,2304]{0,1:T(8,128)(2,1)} %copy.81) | data formatting | bytes 9437184 | tf_op jit(solution)/shard_map/reshape | solution.py:113
  33.9 5.4 slice_bitcast_fusion
  45.1 24.0 %while.26 = (s32[]{:T(128)}, bf16[2,512,12,64]{1,3,2,0:T(8,128)(2,1)}, f32[2,12,512]{2,1,0:T(8,128)}, bf16[2,512,12,64]{1,3,2,0:T(8,128)(2,1)}, pred[2,512]{1,0:...) while((s32[]{:T(128)}, ...), condition=%wide.region_3.4_spmd, body=%wide.region_0.3_spmd.sunk | while | flops 843048960 | bytes 48607928 | solution.py:115
  45.1 4.3 fusion.130
  49.5 2.6 fusion.131
  52.1 4.2 bitcast_dynamic-update-slice_fusion.10
  56.9 4.3 fusion.130
  61.2 2.6 fusion.131
  63.9 4.2 bitcast_dynamic-update-slice_fusion.10
  69.2 3.2 copy.85
  75.8 35.1 %multiply_convert_fusion.1 = (bf16[1024,3072]{1,0:T(8,128)(2,1)S(1)}, f32[1024,3072]{1,0:T(8,128)}, f32[1024,3072]{1,0:T(8,128)}) fusion(f32[3072]{0:T(1024)S(1)} %copy-done.55, bf16[768,3072]{1,0:T(8,128)(2,1)S(1)} %bitcast.215, f32[1024,768]{1,0:T(8,128)S(1)} %get-tuple-element.327, f32[768]{0:T(1024)S(1)} %copy-done.35, f32[768]{0:T(1024)S(1)} %copy-done.30, ...), kind=kOutput, calls=%fused_computation.58 | convolution fusion | flops 5043388416 | bytes 39348224 | tf_op jit(solution)/shard_map/dot_general | solution.py:121
  111.0 5.5 fusion.85
  118.0 6.2 all_gather.6
  124.2 31.4 %all_gather.7 = f32[4,16,768]{2,0,1:T(4,128)S(1)} all-gather(f32[4,2,768]{2,0,1:T(4,128)S(1)} %copy.86), channel_id=1, replica_groups=mesh['dp'=8,'tower'=4] {'dp'}, dimensions={1}, use_global_device_ids=true | all-gather | bytes 221184 | tf_op jit(solution)/shard_map/all_gather | solution.py:130
  175.6 3.7 fusion.54
  181.0 2.4 convert_reduce_fusion.2
  183.4 18.8 %convert_reduce_fusion = (f32[3072]{0:T(1024)}, bf16[1024,3072]{1,0:T(8,128)(2,1)}) fusion(f32[1024,3072]{1,0:T(8,128)} %get-tuple-element.299, bf16[1024,768]{1,0:T(8,128)(2,1)} %get-tuple-element.289, bf16[3072,768]{1,0:T(8,128)(2,1)} %param.32, f32[1024,3072]{1,0:T(8,128)} %get-tuple-element.328, f32[3072]{0:T(1024)S(1)} %copy-done.56), kind=kOutput, calls=%fused_computation.56 | convolution fusion | flops 4885312512 | bytes 37773312 | tf_op jit(solution)/shard_map/td,fd->tf/dot_general | solution.py:143
  202.3 10.7 %multiply_reduce_fusion.2 = (f32[768]{0:T(1024)}, f32[1024]{0:T(1024)S(1)}, f32[768]{0:T(1024)}, f32[1024,768]{1,0:T(8,128)S(1)}) fusion(f32[1024,768]{1,0:T(8,128)S(1)} %copy-done.6, f32[1024]{0:T(1024)S(1)} %fusion.62, f32[1024]{0:T(1024)S(1)} %broadcast_multiply_fusion.3, f32[768]{0:T(1024)S(1)} %copy-done.30, ...), kind=kOutput, calls=%fused_computation.87 | convolution fusion | flops 4839699456 | bytes 20472832 | tf_op jit(solution)/shard_map/tf,df->td/dot_general | solution.py:147
  213.0 8.5 %fusion.73 = f32[768,3072]{1,0:T(8,128)} fusion(bf16[1024,3072]{1,0:T(8,128)(2,1)S(1)} %copy-done.12, f32[1024,768]{1,0:T(8,128)S(1)} %copy-done.6, f32[768]{0:T(1024)S(1)} %copy-done.36, f32[768]{0:T(1024)S(1)} %copy-done.30, f32[1024]{0:T(1024)S(1)} %fusion.62, f32[1024]{0:T(1024)S(1)} %broadcast_multiply_fusion.3), kind=kOutput, calls=%fused_computation.166 | convolution fusion | flops 4835770368 | bytes 18888704 | tf_op jit(solution)/shard_map/td,tf->df/dot_general | solution.py:145
  225.8 2.8 fusion.87
  228.7 2.6 convolution_convert_fusion
  231.2 7.7 fusion.88
  238.9 2.6 copy.89
  241.5 3.8 reshape.321
  245.4 2.9 copy.92
  252.3 52.8 %while.27 = (s32[]{:T(128)}, bf16[2,512,12,64]{1,3,2,0:T(8,128)(2,1)}, bf16[2,512,12,64]{1,3,2,0:T(8,128)(2,1)}, bf16[2,512,12,64]{1,3,2,0:T(8,128)(2,1)}, bf16[...) while((s32[]{:T(128)}, ...), condition=%wide.region_25.26_spmd, body=%wide.region_23.25_spmd.sunk | while | flops 2061232128 | bytes 167706544 | solution.py:160
  253.3 3.4 fusion.140
  256.7 3.1 bitcast_dynamic-update-slice_fusion.14
  259.8 7.4 multiply_reduce_fusion.11
  267.1 7.3 multiply_convert_fusion.3
  279.6 3.4 fusion.140
  283.0 3.1 bitcast_dynamic-update-slice_fusion.14
  286.1 7.3 multiply_reduce_fusion.11
  293.4 7.3 multiply_convert_fusion.3
  305.1 5.2 convert_reduce_fusion.1
  310.3 9.4 %copy.94 = bf16[2,512,3,12,64]{1,0,4,3,2:T(2,128)(2,1)} copy(bf16[2,512,3,12,64]{1,4,3,0,2:T(8,128)(2,1)} %get-tuple-element.293) | data formatting | bytes 9437184 | tf_op jit(solution)/shard_map/convert_element_type | solution.py:166
  319.7 4.0 copy.104
  323.7 2.2 copy-done.19
  325.9 5.8 convolution_bitcast_fusion
  338.0 43.5 %all-reduce.2 = (f32[768]{0:T(1024)}, f32[768]{0:T(1024)}, f32[768]{0:T(1024)}, f32[768]{0:T(1024)}, f32[768]{0:T(1024)}, /*index=5*/f32[3072]{0:T(1024)}, f32[768]{0:T(1024)}, f32[768]{0:T(1024)}, f32[768]{0:T(1024)}) all-reduce(f32[768]{0:T(1024)} %slice.33, f32[768]{0:T(1024)} %slice.35, ...), channel_id=1, replica_groups=mesh['dp'=8,'tower'=4] {'dp','tower'}, use_global_device_ids=true, to_apply=%region_28.29 | all-reduce | flops 9216 | bytes 73728 | tf_op jit(solution)/shard_map/psum | solution.py:175
  381.5 8.6 %add_add_fusion.4 = f32[1024,768]{1,0:T(8,128)} fusion(f32[1024,768]{1,0:T(8,128)} %copy-done.11, bf16[1024,2304]{0,1:T(8,128)(2,1)} %bitcast.202, bf16[768,2304]{1,0:T(8,128)(2,1)S(1)} %copy-done, f32[1024]{0:T(1024)} %copy-done.46), kind=kOutput, calls=%fused_computation.97 | convolution fusion | flops 3625451520 | bytes 14553088 | tf_op jit(solution)/shard_map/te,de->td/dot_general | solution.py:172
  390.1 376.1 %all-reduce.6.cloned.1.call-done = (f32[768,2304]{0,1:T(8,128)}, f32[768,768]{1,0:T(8,128)}, f32[768,3072]{1,0:T(8,128)}, f32[3072,768]{1,0:T(8,128)}) async-done(((f32[768,2304]{0,1:T(8,128)}, f32[768,768]{1,0:T(8,128)}, f32[768,3072]{1,0:T(8,128)}, f32[3072,768]{1,0:T(8,128)}), (f32[768,2304]{0,1:T(8,128)}, f32[768,768]{1,0:T(8,128)}, f32[768,3072]{1,0:T(8,128)}, ...) | async-done | bytes 28311568 | tf_op jit(solution)/shard_map/psum | solution.py:175
  766.2 8.0 copy.95
  774.2 3.4 copy.143
  777.5 8.8 %copy.144 = f32[768,3072]{1,0:T(8,128)} copy(f32[768,3072]{1,0:T(8,128)} %get-tuple-element.520) | data formatting | bytes 18874368
  786.3 3.7 copy.145
  (239 shorter events, 61.6 us)
Async XLA Ops:
  7.2 4.0 copy-start
  7.2 759.0 %all-reduce.6.cloned.1.call-start = ((), (), s32[]{:S(2)}) async-start(), calls=%async_computation | async-start | bytes 56623104 | tf_op jit(solution)/shard_map/psum | solution.py:175
  52.1 4.2 copy-start.24
  63.8 4.2 copy-start.24
  69.1 5.4 copy-start.26
  69.1 3.7 copy-start.51
  69.1 3.7 copy-start.53
  69.2 3.7 copy-start.57
  69.2 6.6 slice-start.5
  72.9 38.0 %slice-start.3 = ((s8[4718592]{0:T(1024)(128)(4,1)}), s8[4194304]{0:T(1024)(128)(4,1)S(1)}, s32[]{:S(2)}) async-start(s8[4718592]{0:T(1024)(128)(4,1)} %bitcast.212), calls=%async_computation.4 | async-start | bytes 8388608
  74.6 36.3 %copy-start.5 = (f32[1024,768]{1,0:T(8,128)}, f32[1024,768]{1,0:T(8,128)S(1)}, u32[]{:S(2)}) copy-start(f32[1024,768]{1,0:T(8,128)S(1)} %get-tuple-element.327) | copy-start | bytes 9437188
  75.8 35.1 %slice-start.4 = ((s8[4718592]{0:T(1024)(128)(4,1)}), s8[524288]{0:T(1024)(128)(4,1)S(1)}, s32[]{:S(2)}) async-start(s8[4718592]{0:T(1024)(128)(4,1)} %bitcast.212), calls=%async_computation.5 | async-start | bytes 1048576
  75.8 35.1 %copy-start.58 = (f32[768]{0:T(1024)S(1)}, f32[768]{0:T(1024)}, u32[]{:S(2)}) copy-start(f32[768]{0:T(1024)} %param.33) | copy-start | bytes 9220
  110.9 5.5 copy-start.59
  110.9 6.1 copy-start.33
  110.9 6.1 copy-start.38
  110.9 6.1 copy-start.47
  116.4 40.6 %copy-start.3 = (f32[1024,768]{1,0:T(8,128)}, f32[1024,768]{1,0:T(8,128)S(1)}, u32[]{:S(2)}) copy-start(f32[1024,768]{1,0:T(8,128)S(1)} %get-tuple-element.330) | copy-start | bytes 9437188
  117.0 40.6 %copy-start.42 = (f32[1024]{0:T(1024)}, f32[1024]{0:T(1024)S(1)}, u32[]{:S(2)}) copy-start(f32[1024]{0:T(1024)S(1)} %multiply_reduce_fusion.5) | copy-start | bytes 12292
  117.0 40.6 %copy-start.31 = (f32[1024]{0:T(1024)}, f32[1024]{0:T(1024)S(1)}, u32[]{:S(2)}) copy-start(f32[1024]{0:T(1024)S(1)} %fusion.63) | copy-start | bytes 12292
  163.6 8.9 %copy-start.44 = (f32[32]{0:T(128)}, f32[32]{0:T(128)S(1)}, u32[]{:S(2)}) copy-start(f32[32]{0:T(128)S(1)} %get-tuple-element.331) | copy-start | bytes 388
  173.6 5.6 copy-start.43
  173.6 5.6 copy-start.4
  173.6 5.6 copy-start.32
  173.6 5.6 copy-start.34
  173.6 5.6 copy-start.37
  175.6 5.4 copy-start.28
  183.4 18.8 %copy-start.6 = (f32[1024,768]{1,0:T(8,128)S(1)}, f32[1024,768]{1,0:T(8,128)}, u32[]{:S(2)}) copy-start(f32[1024,768]{1,0:T(8,128)} %copy-done.5) | copy-start | bytes 9437188
  202.3 10.8 %copy-start.12 = (bf16[1024,3072]{1,0:T(8,128)(2,1)S(1)}, bf16[1024,3072]{1,0:T(8,128)(2,1)}, u32[]{:S(2)}) copy-start(bf16[1024,3072]{1,0:T(8,128)(2,1)} %get-tuple-element.339) | copy-start | bytes 18874372
  202.3 10.8 %copy-start.36 = (f32[768]{0:T(1024)S(1)}, f32[768]{0:T(1024)}, u32[]{:S(2)}) copy-start(f32[768]{0:T(1024)} %param.29) | copy-start | bytes 9220
  213.0 8.5 %copy-start.41 = (f32[1024]{0:T(1024)S(1)}, f32[1024]{0:T(1024)}, u32[]{:S(2)}) copy-start(f32[1024]{0:T(1024)} %copy-done.40) | copy-start | bytes 12292
  223.3 5.4 copy-start.11
  223.3 5.3 copy-start.46
  225.8 5.4 slice-start.7
  245.4 6.9 copy-start.27
  259.8 7.4 copy-start.14
  267.1 7.3 copy-start.1
  267.1 7.3 copy-start.15
  286.1 7.4 copy-start.14
  293.4 7.3 copy-start.1
  293.4 7.3 copy-start.15
  319.7 6.2 copy-start.52
  331.8 4.1 copy-start.45
  331.8 6.0 copy-start.29
  331.8 6.0 copy-start.39
  774.2 12.1 %slice-start = ((s8[9437184]{0:T(1024)(128)(4,1)}), s8[4194304]{0:T(1024)(128)(4,1)S(1)}, s32[]{:S(2)}) async-start(s8[9437184]{0:T(1024)(128)(4,1)} %bitcast.195), calls=%async_computation.1 | async-start | bytes 8388608
  777.5 8.8 %slice-start.1 = ((s8[9437184]{0:T(1024)(128)(4,1)}), s8[4194304]{0:T(1024)(128)(4,1)S(1)}, s32[]{:S(2)}) async-start(s8[9437184]{0:T(1024)(128)(4,1)} %bitcast.195), calls=%async_computation.2 | async-start | bytes 8388608
  777.5 8.8 %slice-start.2 = ((s8[9437184]{0:T(1024)(128)(4,1)}), s8[1048576]{0:T(1024)(128)(4,1)S(1)}, s32[]{:S(2)}) async-start(s8[9437184]{0:T(1024)(128)(4,1)} %bitcast.195), calls=%async_computation.3 | async-start | bytes 2097152
  (35 other events, 75.5 us)
Sparse Core Ops, SparseCore 0:
  331.9 434.2 all-reduce.5
where the time goes:
time: 808 us; the launch traced here: 798 us
  waiting for transfers between devices  376 us (47%)
  matrix products  169 us (21%)
  local copies, waits for them, and re-layouts  99.7 us (12%)
  blocking collectives  81.1 us (10%)
  other arithmetic  54.3 us (7%)
  between operations  16.7 us (2%)
    psum x1, waiting for transfers between devices, local(): lax.psum((grad_w_qkv, grad_q_bias, grad_v_bias, grad_w_out, grad_out_bias...  376 us
    psum x1, blocking collectives, local(): lax.psum((grad_w_qkv, grad_q_bias, grad_v_bias, grad_w_out, grad_out_bias...  43.5 us
    dot_general x1, matrix products, local(): jnp.dot(hidden_low, w_up, preferred_element_type=jnp.float32) + up_bias  35.1 us
    unnamed x119, local copies, waits for them, and re-layouts  34 us
    all_gather x1, blocking collectives, local(): everything = lax.all_gather(grouped, 'dp', axis=1, tiled=True)  31.4 us
    dot_general x1, matrix products, local(): jnp.einsum('td,fd->tf', grad_down, w_down, preferred_element_type=jnp.flo...  18.8 us
  transfers between devices with their start and end apart: 1, of which 1 were waited for; matrix products, arithmetic and copies ran while one was open for 2% of the time, Pallas kernels for 0%

commit v1 on v0

v1 whole, which is shorter than its diff:
```python
from functools import partial

import jax
import jax.numpy as jnp
from jax import lax
from jax.experimental import pallas as pl
from jax.experimental.pallas import tpu as pltpu
from jax.sharding import PartitionSpec as P

HD = 64
SOFTMAX_TEMP = 0.01
NORM_EPS = 1e-06
MASKED = -1e30
F32 = jnp.float32
BF16 = jnp.bfloat16
ROOT_HALF = 0.7071067811865476
INV_ROOT_2PI = 0.3989422804014327
MIB = 1024 * 1024

SMEM = pl.BlockSpec(memory_space=pltpu.SMEM)
VMEM = pl.BlockSpec(memory_space=pltpu.VMEM)
ANY = pl.BlockSpec(memory_space=pl.ANY)


LIGHT = pl.CostEstimate(flops=1, bytes_accessed=1, transcendentals=0)


def params():
    return pltpu.CompilerParams(vmem_limit_bytes=62 * MIB)


def call(body, dep, grid, in_specs, out_specs, out_shape, scratch=(), scalars=0, name=None):
    n_in = scalars + len(in_specs)

    def run(*refs):
        if dep is None:
            return body(*refs)
        return body(*refs[:n_in], *refs[n_in + 1:])

    spec = pltpu.PrefetchScalarGridSpec(
        num_scalar_prefetch=scalars, grid=grid, in_specs=list(in_specs) + ([] if dep is None else [ANY]),
        out_specs=out_specs, scratch_shapes=scratch)
    made = pl.pallas_call(run, grid_spec=spec, out_shape=out_shape, compiler_params=params(), cost_estimate=LIGHT, name=name)
    return made if dep is None else lambda *args: made(*args, dep)


def shape(dims, kind):
    return jax.ShapeDtypeStruct(dims, kind)


def line(cols, index=lambda *_: (0,)):
    return pl.BlockSpec((cols,), index)


def row(ref):
    return ref[...].reshape(1, -1)


def fixed(dims):
    return pl.BlockSpec(dims, lambda *_: (0,) * len(dims), pipeline_mode=pl.Buffered(1))


def dot(a, b, ca=1, cb=0):
    return lax.dot_general(a, b, (((ca,), (cb,)), ((), ())), preferred_element_type=F32)


def key_mask(count, span):
    place = lax.broadcasted_iota(jnp.int32, (span, 1), 0)
    return jnp.where(place < count, 0.0, MASKED)


def attend_body(seqs, span, group, counts, x, wq, wk, wv, qb, vb, q_out, k_out, v_out, ctx, lse):
    q_out[...] = (dot(x[...], wq[...]) + row(qb)).astype(BF16)
    k_out[...] = dot(x[...], wk[...]).astype(BF16)
    v_out[...] = (dot(x[...], wv[...]) + row(vb)).astype(BF16)
    for s in range(seqs):
        rows = pl.ds(s * span, span)
        mask = key_mask(counts[0, s], span)
        for pair in range(group // 2):
            both = []
            for half in range(2):
                head = pair * 2 + half
                lanes = pl.ds(head * HD, HD)
                query = q_out[rows, lanes] * HD ** (-0.5)
                scores = dot(k_out[rows, lanes], query, 1, 1) + mask
                highest = jnp.max(scores, axis=0, keepdims=True)
                expo = jnp.exp(scores - highest)
                summed = jnp.sum(expo, axis=0, keepdims=True)
                probs = (expo * (1.0 / summed)).astype(BF16)
                both.append(dot(v_out[rows, lanes], probs, 0, 0))
                lse[0, s, pl.ds(head, 1), :] = highest + jnp.log(summed)
            both = jnp.concatenate(both, axis=0)
            ctx[rows, pl.ds(pair * 2 * HD, 2 * HD)] = both.T.astype(BF16)


def attend(counts, x, w_qkv, q_bias, v_bias, seqs, span):
    rows, width = x.shape
    group = 4
    cols = group * HD
    steps = width // cols
    piece = pl.BlockSpec((rows, cols), lambda g: (0, g))
    bias = line(cols, lambda g: (g,))
    weight = [pl.BlockSpec((width, cols), lambda g, k=k: (0, k * steps + g)) for k in range(3)]
    return pl.pallas_call(
        partial(attend_body, seqs, span, group),
        grid=(steps,),
        in_specs=[SMEM, fixed((rows, width)), *weight, bias, bias],
        out_specs=[piece] * 4 + [pl.BlockSpec((1, seqs, group, span), lambda g: (g, 0, 0, 0))],
        out_shape=[shape((rows, width), BF16)] * 4 + [shape((steps, seqs, group, span), F32)],
        compiler_params=params(),
        cost_estimate=LIGHT,
        name="attend",
    )(counts, x, w_qkv, w_qkv, w_qkv, q_bias, v_bias)


def norm_parts(value):
    centre = value - jnp.mean(value, axis=-1, keepdims=True)
    spread = jnp.mean(centre * centre, axis=-1, keepdims=True)
    scale = lax.rsqrt(spread + NORM_EPS)
    return centre * scale, scale


def gelu_parts(u):
    a = jnp.abs(u)
    t = 1.0 / (1.0 + (0.3275911 * ROOT_HALF) * a)
    poly = t * (0.254829592 + t * (-0.284496736 + t * (1.421413741 + t * (-1.453152027 + t * 1.061405429))))
    bell = jnp.exp(-0.5 * (u * u))
    tail = (0.5 * poly) * bell
    cdf = jnp.where(u >= 0.0, 1.0 - tail, tail)
    return u * cdf, cdf + u * (INV_ROOT_2PI * bell)


def feed_body(tile, span, chunk, counts, x, ctx, w_out, w_up, w_down, ob, g1, b1, ub, db,
              hid_t, hat1, sc1, act, slope, hat2, sc2, sums):
    step = pl.program_id(0)
    attn = dot(ctx[...], w_out[...]) + row(ob)
    xhat, scale = norm_parts(x[...].astype(F32) + attn)
    hat1[...] = xhat
    sc1[...] = scale
    hidden = xhat * row(g1) + row(b1)
    low = hidden.astype(BF16)
    hid_t[...] = low.T
    total = hidden + row(db)
    for j in range(w_up.shape[1] // chunk):
        cols = pl.ds(j * chunk, chunk)
        upper = dot(low, w_up[:, cols]) + ub[cols].reshape(1, chunk)
        active, grad = gelu_parts(upper)
        active = active.astype(BF16)
        act[:, cols] = active
        slope[:, cols] = grad.astype(slope.dtype)
        total = total + dot(active, w_down[cols, :])
    xhat, scale = norm_parts(total)
    hat2[...] = xhat
    sc2[...] = scale
    seq = step * tile // span
    place = lax.broadcasted_iota(jnp.int32, (tile, 1), 0) + lax.rem(step * tile, span)
    part = jnp.sum(jnp.where(place < counts[0, seq], xhat, 0.0), axis=0, keepdims=True)

    @pl.when(step == 0)
    def _():
        sums[...] = jnp.zeros_like(sums)

    sums[pl.ds(seq, 1), :] += part


def feed(counts, x, ctx, w_out, w_up, w_down, ob, g1, b1, ub, db, seqs, span, slope_kind):
    rows, width = x.shape
    ff = w_up.shape[1]
    tile = 256
    by = lambda cols: pl.BlockSpec((tile, cols), lambda i: (i, 0))
    return pl.pallas_call(
        partial(feed_body, tile, span, 768),
        grid=(rows // tile,),
        in_specs=[SMEM, by(width), by(width), fixed((width, width)), fixed((width, ff)), fixed((ff, width)),
                  line(width), line(width), line(width), line(ff), line(width)],
        out_specs=[pl.BlockSpec((width, tile), lambda i: (0, i)), by(width), by(1), by(ff), by(ff), by(width), by(1),
                   pl.BlockSpec((seqs, width), lambda i: (0, 0))],
        out_shape=[shape((width, rows), BF16), shape((rows, width), F32), shape((rows, 1), F32),
                   shape((rows, ff), BF16), shape((rows, ff), slope_kind), shape((rows, width), F32),
                   shape((rows, 1), F32), shape((seqs, width), F32)],
        compiler_params=params(),
        cost_estimate=LIGHT,
        name="feed",
    )(counts, x, ctx, w_out, w_up, w_down, ob, g1, b1, ub, db)


def loss_body(n_dp, towers, seqs, span, bits, counts, own, pos, every, sums, g2, hat2, sc2,
              loss, dres, ddown, small, scratch):
    count = n_dp * towers * seqs
    pairs = pos.shape[0]
    rows = every[...]
    inv = lax.rsqrt(jnp.sum(rows * rows, axis=-1, keepdims=True) + NORM_EPS)
    unit = rows * inv
    full = lax.Precision.HIGHEST
    logits = lax.dot_general(unit, unit, (((1,), (1,)), ((), ())), precision=full,
                             preferred_element_type=F32) / SOFTMAX_TEMP

    def place(i):
        block, j = i // seqs, lax.rem(i, seqs)
        device = jnp.full_like(block, own[0, 0])
        for n, bit in enumerate(bits):
            device = device ^ (((block >> n) & 1) * bit)
        dp, tower = device // towers, lax.rem(device, towers)
        half = towers // 2
        return tower < half, lax.rem(tower, half) * (n_dp * seqs) + dp * seqs + j

    is_query, query = place(lax.broadcasted_iota(jnp.int32, (count, 1), 0))
    key_is_query, key = place(lax.broadcasted_iota(jnp.int32, (1, count), 1))
    is_key = jnp.logical_not(key_is_query)
    lookup = lax.broadcasted_iota(jnp.int32, (count, pairs), 1) == query
    wanted = jnp.sum(jnp.where(lookup, row(pos).astype(F32), 0.0), axis=1, keepdims=True)
    hit = (key.astype(F32) == wanted) & is_key & is_query
    inside = is_key & is_query
    shown = jnp.where(is_key, logits, MASKED)
    highest = jnp.max(shown, axis=1, keepdims=True)
    expo = jnp.where(inside, jnp.exp(shown - highest), 0.0)
    summed = jnp.sum(expo, axis=1, keepdims=True)
    safe = jnp.where(is_query, summed, 1.0)
    picked = jnp.sum(jnp.where(hit, logits, 0.0), axis=1, keepdims=True)
    each = jnp.where(is_query, highest + jnp.log(safe) - picked, 0.0)
    loss[...] = jnp.sum(each, axis=0, keepdims=True) / pairs
    grad = (expo / safe - jnp.where(hit, 1.0, 0.0)) / (pairs * SOFTMAX_TEMP)
    dunit = lax.dot_general(grad, unit, (((1,), (0,)), ((), ())), precision=full, preferred_element_type=F32)
    dunit += lax.dot_general(grad, unit, (((0,), (0,)), ((), ())), precision=full, preferred_element_type=F32)
    inner = jnp.sum(dunit * rows, axis=-1, keepdims=True)
    scratch[...] = inv * dunit - rows * (inv * inv * inv * inner)

    width = rows.shape[1]
    small[...] = jnp.zeros_like(small)
    for s in range(seqs):
        pooled = scratch[pl.ds(s, 1), :]
        n = counts[0, s]
        dout = pooled / n.astype(F32)
        small[0:1, :] += dout * sums[s:s + 1, :]
        small[1:2, :] += pooled
        dhat = dout * row(g2)
        first = jnp.mean(dhat, axis=-1, keepdims=True)
        total = jnp.zeros((1, width), F32)
        tile = span // 2
        for part in range(2):
            at = pl.ds(s * span + part * tile, tile)
            xhat = hat2[at, :]
            second = jnp.mean(dhat * xhat, axis=-1, keepdims=True)
            live = lax.broadcasted_iota(jnp.int32, (tile, 1), 0) + part * tile < n
            scale = jnp.where(live, sc2[at, :], 0.0)
            value = scale * (dhat - first - xhat * second)
            dres[at, :] = value
            low = value.astype(BF16)
            ddown[at, :] = low
            total += jnp.sum(low.astype(F32), axis=0, keepdims=True)
        small[2:3, :] += total


def loss_step(counts, own, pos, every, sums, g2, hat2, sc2, n_dp, towers, seqs, span, bits):
    rows, width = hat2.shape
    return pl.pallas_call(
        partial(loss_body, n_dp, towers, seqs, span, bits),
        in_specs=[SMEM, SMEM] + [VMEM] * 6,
        out_specs=[VMEM] * 4,
        out_shape=[shape((1, 1), F32), shape((rows, width), F32), shape((rows, width), BF16), shape((8, width), F32)],
        scratch_shapes=[pltpu.VMEM(every.shape, F32)],
        compiler_params=params(),
        cost_estimate=LIGHT,
        name="loss",
    )(counts, own, pos, every, sums, g2, hat2, sc2)


def slope_body(ddown, slope, w_down, dupper, upb):
    value = (slope[...].astype(F32) * dot(ddown[...], w_down[...], 1, 1)).astype(BF16)
    dupper[...] = value
    upb[...] = jnp.sum(value.astype(F32), axis=0, keepdims=True)


def slope_back(ddown, slope, w_down, dep):
    rows, width = ddown.shape
    ff = slope.shape[1]
    tile = 512
    by = pl.BlockSpec((rows, tile), lambda i: (0, i))
    return call(
        slope_body, dep, (ff // tile,), [fixed((rows, width)), by, pl.BlockSpec((tile, width), lambda i: (i, 0))],
        [by, pl.BlockSpec((1, tile), lambda i: (0, i))], [shape((rows, ff), BF16), shape((1, ff), F32)],
        name="slope_back",
    )(ddown, slope, w_down)


def share(value, j, place, send, keep):
    rows = value.shape[0]

    @pl.when(place[j] < 2)
    def _():
        send[pl.ds(pl.multiple_of(place[j] * rows, rows), rows), :] = value

    @pl.when(place[j] >= 2)
    def _():
        keep[pl.ds(pl.multiple_of((place[j] - 2) * rows, rows), rows), :] = value


def up_send_body(which, a0, a1, a2, a3, b, out):
    out[...] = dot(jnp.concatenate([a0[...], a1[...], a2[...], a3[...]], axis=0), b[...])


def up_keep_body(which, place, a0, a1, a2, a3, b, came, send, keep):
    value = dot(jnp.concatenate([a0[...], a1[...], a2[...], a3[...]], axis=0), b[...])
    rows = a0.shape[0]
    for j in range(4):
        at = pl.ds(j * rows, rows)
        share(value[j * rows:(j + 1) * rows] + came[at, :], j, place, send, keep)


def up_grad(which, a, b, place=None, came=None, dep=None):
    m, k = a.shape
    n = b.shape[1]
    rows, tile = m // 8, 512
    ins = [pl.BlockSpec((rows, k), lambda i, w, *_, j=j: (2 * j + w[0], 0)) for j in range(4)]
    ins.append(pl.BlockSpec((k, tile), lambda i, *_: (0, i)))
    by = lambda r: pl.BlockSpec((r, tile), lambda i, *_: (0, i))
    if came is None:
        return call(up_send_body, dep, (n // tile,), ins, by(m // 2), shape((m // 2, n), F32), scalars=1,
                    name="up_send")(which, a, a, a, a, b)
    return call(up_keep_body, dep, (n // tile,), ins + [by(m // 2)], [by(m // 4)] * 2,
                [shape((m // 4, n), F32)] * 2, scalars=2, name="up_keep")(which, place, a, a, a, a, b, came)


def down_send_body(which, a, b, out):
    out[...] = dot(a[...], b[...], 0, 0)


def down_keep_body(which, order, a, b, came, send, keep):
    value = dot(a[...], b[...], 0, 0) + came[...]
    step = pl.program_id(0)

    @pl.when(step < 2)
    def _():
        send[...] = value

    @pl.when(step >= 2)
    def _():
        keep[...] = value


def down_grad(which, a, b, order=None, came=None, dep=None):
    rows, m = a.shape
    n = b.shape[1]
    tile = m // 8
    block = (tile, n)
    if came is None:
        return call(down_send_body, dep, (4,),
                    [pl.BlockSpec((rows, tile), lambda i, w: (0, 2 * i + w[0])), fixed((rows, n))],
                    pl.BlockSpec(block, lambda i, w: (i, 0)), shape((m // 2, n), F32), scalars=1,
                    name="down_send")(which, a, b)
    return call(down_keep_body, dep, (4,),
                [pl.BlockSpec((rows, tile), lambda i, w, o: (0, 2 * o[i] + w[0])), fixed((rows, n)),
                 pl.BlockSpec(block, lambda i, w, o: (o[i], 0))],
                [pl.BlockSpec(block, lambda i, w, o: (jnp.minimum(i, 1), 0)),
                 pl.BlockSpec(block, lambda i, w, o: (jnp.maximum(i - 2, 0), 0))],
                [shape((m // 4, n), F32)] * 2, scalars=2, name="down_keep")(which, order, a, b, came)


MORE = 16


def last_products(x, ctx, dattn, parts):
    span = parts[0].shape[0]
    seqs = len(parts) // 3
    for kind in range(3):
        value = None
        for s in range(seqs):
            term = dot(x[pl.ds(s * span, span), :], parts[s * 3 + kind][...], 0, 0)
            value = term if value is None else value + term
        yield value
    yield dot(ctx[...], dattn[...], 0, 0)


def last_small(which, small, kind):
    if kind:
        return jnp.zeros(small.shape, F32)
    return jnp.where(which[0] == 0, small[...], 0.0)


def last_send_body(which, x, ctx, dattn, small, *rest):
    parts, out = rest[:-1], rest[-1]
    rows = x.shape[1]
    for kind, value in enumerate(last_products(x, ctx, dattn, parts)):
        at = kind * (rows + MORE)
        out[pl.ds(at, rows), :] = value
        out[pl.ds(at + rows, MORE), :] = last_small(which, small, kind)


def last_keep_body(which, place, x, ctx, dattn, small, came, *rest):
    parts, send, keep = rest[:-2], rest[-2], rest[-1]
    rows = x.shape[1]
    size = rows + MORE
    for kind, value in enumerate(last_products(x, ctx, dattn, parts)):
        at = kind * size
        value = value + came[pl.ds(at, rows), :]
        more = last_small(which, small, kind) + came[pl.ds(at + rows, MORE), :]

        def put(out, spot):
            start = pl.multiple_of(spot * size, 8)
            out[pl.ds(start, rows), :] = value
            out[pl.ds(pl.multiple_of(start + rows, 8), MORE), :] = more

        pl.when(place[kind] < 2)(lambda: put(send, place[kind]))
        pl.when(place[kind] >= 2)(lambda: put(keep, place[kind] - 2))


def last_grad(which, x, ctx, dattn, small, parts, place=None, came=None, dep=None):
    rows, width = x.shape
    half = width // 2
    size = half + MORE
    whole = lambda v: pl.BlockSpec(v.shape, lambda i, *_: (0, 0), pipeline_mode=pl.Buffered(1))
    part = pl.BlockSpec((rows, half), lambda i, w, *_: (0, w[0]), pipeline_mode=pl.Buffered(1))
    out = lambda r: pl.BlockSpec((r, width), lambda i, *_: (0, 0), pipeline_mode=pl.Buffered(1))
    ins = [part, part, whole(dattn), whole(small)]
    if came is None:
        return call(last_send_body, dep, (1,), ins + [whole(v) for v in parts], out(4 * size),
                    shape((4 * size, width), F32), scalars=1, name="last_send")(which, x, ctx, dattn, small, *parts)
    return call(last_keep_body, dep, (1,), ins + [whole(came)] + [whole(v) for v in parts], [out(2 * size)] * 2,
                [shape((2 * size, width), F32)] * 2, scalars=2, name="last_keep")(
                    which, place, x, ctx, dattn, small, came, *parts)


def middle_body(dupper, w_up, dres, hat1, sc1, g1, w_out, dres1, dattn, dctx, small):
    dhid = dres[...] + dot(dupper[...], w_up[...], 1, 1)
    xhat = hat1[...]

    @pl.when(pl.program_id(0) == 0)
    def _():
        small[...] = jnp.zeros_like(small)

    small[1:2, :] += jnp.sum(dhid * xhat, axis=0, keepdims=True)
    small[2:3, :] += jnp.sum(dhid, axis=0, keepdims=True)
    dhat = dhid * row(g1)
    first = jnp.mean(dhat, axis=-1, keepdims=True)
    second = jnp.mean(dhat * xhat, axis=-1, keepdims=True)
    value = sc1[...] * (dhat - first - xhat * second)
    dres1[...] = value
    low = value.astype(BF16)
    dattn[...] = low
    small[0:1, :] += jnp.sum(low.astype(F32), axis=0, keepdims=True)
    dctx[...] = dot(low, w_out[...], 1, 1).astype(BF16)


def middle_back(dupper, w_up, dres, hat1, sc1, g1, w_out, dep):
    rows, width = dres.shape
    ff = dupper.shape[1]
    tile = 256
    by = lambda cols: pl.BlockSpec((tile, cols), lambda i: (i, 0))
    return call(
        middle_body, dep, (rows // tile,),
        [by(ff), fixed((width, ff)), by(width), by(width), by(1), line(width), fixed((width, width))],
        [by(width), by(width), by(width),
         pl.BlockSpec((8, width), lambda i: (0, 0))],
        [shape((rows, width), F32), shape((rows, width), BF16), shape((rows, width), BF16),
         shape((8, width), F32)], name="middle_back",
    )(dupper, w_up, dres, hat1, sc1, g1, w_out)


def attend_back_body(seq, span, group, counts, q, k, v, dctx, lse, dep, dq, dk, dv, qsum, vsum):
    mask = key_mask(counts[0, seq], span)
    for pair in range(group // 2):
        turned, keys, values = [], [], []
        for half in range(2):
            head = pair * 2 + half
            lanes = pl.ds(head * HD, HD)
            query = q[:, lanes] * HD ** (-0.5)
            key = k[:, lanes]
            grad = dctx[:, lanes]
            scores = dot(key, query, 1, 1) + mask
            probs = jnp.exp(scores - lse[0, 0, pl.ds(head, 1), :])
            dprobs = dot(v[:, lanes], grad, 1, 1)
            values.append(dot(probs.astype(BF16), grad))
            inner = jnp.sum(probs * dprobs, axis=0, keepdims=True)
            dscores = (probs * (dprobs - inner)).astype(BF16)
            keys.append(dot(dscores, query))
            turned.append(dot(key, dscores, 0, 0))
        cols = pl.ds(pair * 2 * HD, 2 * HD)
        low = (jnp.concatenate(turned, axis=0).T * HD ** (-0.5)).astype(BF16)
        dq[:, cols] = low
        qsum[:, cols] = jnp.sum(low.astype(F32), axis=0, keepdims=True)
        dk[:, cols] = jnp.concatenate(keys, axis=1).astype(BF16)
        low = jnp.concatenate(values, axis=1).astype(BF16)
        dv[:, cols] = low
        vsum[:, cols] = jnp.sum(low.astype(F32), axis=0, keepdims=True)


def attend_back(seq, counts, q, k, v, dctx, lse, span, dep):
    width = q.shape[1]
    group = 4
    cols = group * HD
    piece = pl.BlockSpec((span, cols), lambda g: (seq, g))
    mine = pl.BlockSpec((span, cols), lambda g: (0, g))
    line = pl.BlockSpec((1, cols), lambda g: (0, g))
    return pl.pallas_call(
        partial(attend_back_body, seq, span, group),
        grid=(width // cols,),
        in_specs=[SMEM] + [piece] * 4 + [pl.BlockSpec((1, 1, group, span), lambda g: (g, seq, 0, 0)), ANY],
        out_specs=[mine] * 3 + [line] * 2,
        out_shape=[shape((span, width), BF16)] * 3 + [shape((1, width), F32)] * 2,
        compiler_params=params(),
        cost_estimate=LIGHT,
        name="attend_back",
    )(counts, q, k, v, dctx, lse, dep)


def token_body(steps, dres1, wq, wk, wv, dep, *rest):
    parts, out = rest[:-1], rest[-1]
    for s in range(len(parts) // 3):
        at = pl.ds(s * parts[0].shape[0], parts[0].shape[0])
        total = dres1[at, :]
        for part, weight in zip(parts[s * 3:s * 3 + 3], (wq, wk, wv)):
            total = total + dot(part[...], weight[...], 1, 1)
        out[at, :] = total


def token_grad(dres1, w_qkv, parts, dep):
    rows, width = dres1.shape
    span = parts[0].shape[0]
    full = pl.BlockSpec((span, width), lambda i: (0, 0), pipeline_mode=pl.Buffered(1))
    tile = 256
    steps = width // tile
    by = pl.BlockSpec((rows, tile), lambda i: (0, i))
    weight = [pl.BlockSpec((tile, width), lambda i, k=k: (i, k)) for k in range(3)]
    return pl.pallas_call(
        partial(token_body, steps),
        grid=(steps,),
        in_specs=[by, *weight, ANY] + [full] * len(parts),
        out_specs=by,
        out_shape=shape((rows, width), F32),
        compiler_params=params(),
        cost_estimate=LIGHT,
        name="token_grad",
    )(dres1, w_qkv, w_qkv, w_qkv, dep, *parts)


def add_split_body(steps, bit, held, came, send, keep):
    step = pl.program_id(0)
    value = held[...] + came[...]

    @pl.when(step < steps)
    def _():
        send[...] = value

    @pl.when(step >= steps)
    def _():
        keep[...] = value


def block_rows(rows, cols):
    best = 8
    for r in range(8, rows + 1, 8):
        if rows % r == 0 and r * cols * 4 <= MIB:
            best = r
    return best


def add_split(bit, held, came, dep=None):
    rows, cols = held.shape
    half = rows // 2
    tile = block_rows(half, cols)
    steps = half // tile

    def at(i, b):
        first = i < steps
        return jnp.where(first, (1 - b[0]) * steps + i, b[0] * steps + i - steps), 0

    block = (tile, cols)
    return call(
        partial(add_split_body, steps), dep, (2 * steps,), [pl.BlockSpec(block, at)] * 2,
        [pl.BlockSpec(block, lambda i, b: (jnp.minimum(i, steps - 1), 0)),
         pl.BlockSpec(block, lambda i, b: (jnp.maximum(i - steps, 0), 0))],
        [shape((half, cols), F32)] * 2, scalars=1, name="add_split",
    )(bit, held, came)


def add_body(held, came, out):
    out[...] = held[...] + came[...]


def add(held, came, dep=None):
    rows, cols = held.shape
    tile = block_rows(rows, cols)
    spec = pl.BlockSpec((tile, cols), lambda i: (i, 0))
    return call(add_body, dep, (rows // tile,), [spec] * 2, spec, shape((rows, cols), F32), name="add")(held, came)


def gather_body(n, targets, earlier, places, *refs):
    pieces, outs, (held, in_sems, out_sems) = refs[:n], refs[n + earlier:-3], refs[-3:]
    rows = pieces[0].shape[0]
    reads = [pltpu.make_async_copy(piece, held.at[i], in_sems.at[i]) for i, piece in enumerate(pieces)]
    for copy in reads:
        copy.start()

    def each(i, act):
        for kind, first, height, out, column in targets:
            if kind is None:
                at = places[i] * height
            elif kind < 0:
                at = 0
            else:
                at = lax.rem(places[i], 2) * height
            cols = held.shape[2]
            copy = pltpu.make_async_copy(
                held.at[i, pl.ds(first, height), :],
                outs[out].at[pl.ds(pl.multiple_of(at, 8), height), pl.ds(column, cols)],
                out_sems.at[i, 1 if kind is not None and kind < 0 else 0])
            if kind is None:
                act(copy)
            elif kind < 0:
                pl.when(places[i] == 0)(partial(act, copy))
            else:
                pl.when(places[i] // 2 == kind)(partial(act, copy))

    for i in range(n):
        reads[i].wait()
        each(i, lambda copy: copy.start())
    for i in range(n):
        each(i, lambda copy: copy.wait())


def gather(places, pieces, outs, targets, dep=None, into=()):
    n = len(pieces)
    rows, cols = pieces[0].shape
    ins = [SMEM] + [ANY] * (n + len(into))
    body = partial(gather_body, n, targets, len(into))
    n_in = len(ins)

    def run(*refs):
        return body(*refs) if dep is None else body(*refs[:n_in], *refs[n_in + 1:])

    return pl.pallas_call(
        run, in_specs=ins + ([] if dep is None else [ANY]), out_specs=[ANY] * len(outs), out_shape=outs,
        scratch_shapes=[pltpu.VMEM((n, rows, cols), F32), pltpu.SemaphoreType.DMA((n,)),
                        pltpu.SemaphoreType.DMA((n, 2))],
        input_output_aliases={1 + n + k: k for k in range(len(into))},
        compiler_params=params(), cost_estimate=LIGHT, name="gather",
    )(places, *pieces, *into, *([] if dep is None else [dep]))


class Ring:
    def __init__(self, n_dp, towers):
        self.n_dp, self.towers = n_dp, towers
        self.dp, self.tower = lax.axis_index("dp").astype(jnp.int32), lax.axis_index("tower").astype(jnp.int32)
        self.core = self.tower & 1
        x, y = self.x, self.y = self.dp & 1, (self.tower >> 1) & 1
        self.outer = jnp.where(self.core == 0, x, y)
        self.inner = jnp.where(self.core == 0, y, x)
        self.near = (self.dp >> 1) & 1
        self.far = [b for b in (4, 8, 16, 32, 64) if b < n_dp]

    def move(self, value, partner):
        pairs = []
        for dp in range(self.n_dp):
            for tower in range(self.towers):
                to_dp, to_tower = partner(dp, tower)
                pairs.append((dp * self.towers + tower, to_dp * self.towers + to_tower))
        return lax.ppermute(value, ("dp", "tower"), pairs)

    def place(self):
        out = []
        for bx in range(2):
            for by in range(2):
                outer, inner = jnp.where(self.core == 0, bx, by), jnp.where(self.core == 0, by, bx)
                out.append(jnp.where(outer == self.outer, 2, 0) + inner)
        return jnp.stack(out).astype(jnp.int32)

    def order(self):
        out = []
        for outer in (1 - self.outer, self.outer):
            for inner in range(2):
                out.append(jnp.where(self.core == 0, outer * 2 + inner, inner * 2 + outer))
        return jnp.stack(out).astype(jnp.int32)

    def bits(self):
        bits = [1]
        while bits[0] * 2 < self.n_dp * self.towers:
            bits.insert(0, bits[0] * 2)
        return bits

    def to_index(self, value, bit):
        count = self.n_dp * self.towers
        return lax.ppermute(value, ("dp", "tower"), [(i, i ^ bit) for i in range(count)])

    def to_core(self, value):
        return self.move(value, lambda d, t: (d, t ^ 1))

    def to_outer(self, value):
        return self.move(value, lambda d, t: (d, t ^ 2) if t & 1 else (d ^ 1, t))

    def to_inner(self, value):
        return self.move(value, lambda d, t: (d ^ 1, t) if t & 1 else (d, t ^ 2))

    def to_dp(self, value, bit):
        return self.move(value, lambda d, t: (d ^ bit, t))


class Sum:
    def __init__(self, ring, send):
        self.ring = ring
        self.came = ring.to_core(send)

    def s1(self, send, keep):
        self.keep = keep
        self.came = self.ring.to_outer(send)
        return keep

    def s2(self, dep):
        send, self.keep = add_split(self.ring.inner.reshape(1), self.keep, self.came, dep)
        self.came = self.ring.to_inner(send)
        return self.keep

    def s3(self, dep):
        send, self.keep = add_split(self.ring.near.reshape(1), self.keep, self.came, dep)
        self.came = self.ring.to_dp(send, 2)
        return self.keep

    def s4(self, dep):
        self.keep = add(self.keep, self.came, dep)
        for bit in self.ring.far[:-1]:
            self.keep = self.keep + self.ring.to_dp(self.keep, bit)
        self.came = self.ring.to_dp(self.keep, self.ring.far[-1])
        return self.keep

    def s5(self, dep):
        self.keep = add(self.keep, self.came, dep)
        self.came = self.ring.to_dp(self.keep, 2)
        return self.keep

    def s6(self, dep):
        ring = self.ring
        places = jnp.stack([ring.near, 1 - ring.near])
        rows, cols = self.keep.shape
        targets = [(None, 0, rows, 0, 0)]
        (own,) = gather(places, [self.keep, self.came], [shape((2 * rows, cols), F32)], targets, dep)
        self.pieces = [own, ring.to_inner(own), ring.to_outer(own)]
        return own

    def s7(self, outs, targets, dep, into=()):
        ring = self.ring
        own, inner, outer = self.pieces
        mine = [own, inner, outer, ring.to_outer(inner)]
        pieces = mine + [ring.to_core(v) for v in mine]
        c = ring.core
        places = []
        for core in (c, 1 - c):
            inner_step = jnp.where(core == 0, 2, 4)
            base = ring.x * 4 + ring.y * 2
            places += [(base ^ step) + core for step in (0 * inner_step, inner_step, 6 - inner_step, 6 + 0 * inner_step)]
        return gather(jnp.stack(places), pieces, outs, targets, dep, into)


def local(n_dp, towers, tokens, lengths, positive, w_qkv, q_bias, v_bias, w_out, out_bias, norm1_gain, norm1_bias,
          w_up, up_bias, w_down, down_bias, norm2_gain, norm2_bias):
    seqs, span, width = tokens.shape[1:]
    ff = up_bias.shape[0]
    x = tokens.reshape(seqs * span, width)
    ring = Ring(n_dp, towers)
    mine, other = ring.core.reshape(1), (1 - ring.core).reshape(1)
    place = ring.place()
    q, k, v, ctx, lse = attend(lengths, x, w_qkv, q_bias, v_bias, seqs, span)
    hid_t, hat1, sc1, act, slope, hat2, sc2, sums = feed(
        lengths, x, ctx, w_out, w_up, w_down, out_bias, norm1_gain, norm1_bias, up_bias, down_bias, seqs, span, F32)
    pooled = sums * norm2_gain / lengths[0][:, None].astype(F32) + norm2_bias
    every, bits = pooled, ring.bits()
    for bit in bits:
        every = jnp.concatenate([every, ring.to_index(every, bit)], axis=0)
    own = (lax.axis_index("dp") * towers + lax.axis_index("tower")).astype(jnp.int32).reshape(1, 1)
    loss, dres, ddown, small2 = loss_step(lengths, own, positive, every, sums, norm2_gain, hat2, sc2,
                                          n_dp, towers, seqs, span, bits)
    send = down_grad(other, act, ddown)
    down = Sum(ring, send)
    dupper, upb = slope_back(ddown, slope, w_down, send)
    send, keep = down_grad(mine, act, ddown, ring.order(), down.came, dupper)
    dep = down.s1(send, keep)
    send = up_grad(other, hid_t, dupper, dep=dep)
    up = Sum(ring, send)
    dres1, dattn, dctx, small1 = middle_back(dupper, w_up, dres, hat1, sc1, norm1_gain, w_out, send)
    dep = down.s2(dattn)
    send, keep = up_grad(mine, hid_t, dupper, place, up.came, dep)
    dep = up.s1(send, keep)
    back0 = attend_back(0, lengths, q, k, v, dctx, lse, span, dep)
    dep = down.s3(back0[0])
    back1 = attend_back(1, lengths, q, k, v, dctx, lse, span, dep)
    dep = down.s4(back1[0])
    dep = up.s2(dep)
    parts = list(back0[:3] + back1[:3])
    smalls = jnp.concatenate([back0[3] + back1[3], back0[4] + back1[4], small1[:3], upb.reshape(-1, width), small2[:3]], axis=0)
    lines = smalls.shape[0]
    smalls = jnp.pad(smalls, ((0, MORE - lines), (0, 0)))
    send = last_grad(other, x, ctx, dattn, smalls, parts, dep=dep)
    last = Sum(ring, send)
    dep = up.s3(send)
    grad_tokens = token_grad(dres1, w_qkv, parts, dep)
    dep = down.s5(grad_tokens)
    send, keep = last_grad(mine, x, ctx, dattn, smalls, parts, place, last.came, dep)
    dep = last.s1(send, keep)
    dep = up.s4(dep)
    dep = down.s6(dep)
    dep = up.s5(dep)
    dep = last.s2(dep)
    dep = up.s6(dep)
    dep = last.s3(dep)
    dep = last.s4(dep)
    rows = width // 2
    (g1,) = down.s7([shape((ff, width), F32)], [(None, 0, ff // 8, 0, 0)], dep)
    dep = last.s5(g1)
    (g2,) = up.s7([shape((width, ff), F32)], [(None, 0, width // 8, 0, 0)], dep)
    dep = last.s6(g2)
    qkv, out, tail = last.s7(
        [shape((width, 3 * width), F32), shape((width, width), F32), shape((MORE, width), F32)],
        [(0, 0, rows, 0, 0), (1, 0, rows, 0, width), (2, 0, rows, 0, 2 * width), (3, 0, rows, 1, 0), (-1, rows, MORE, 2, 0)],
        dep)
    return outputs(loss, grad_tokens.reshape(tokens.shape), g1, g2, qkv, out, tail[:lines], width)


def outputs(loss, grad_tokens, down, up, qkv, out, smalls, width):
    lines = smalls.reshape(-1, width)
    n = up.shape[1] // width
    return (loss[0, 0], grad_tokens, qkv, lines[0], lines[1], out, lines[2], lines[3], lines[4], up,
            lines[5:5 + n].reshape(-1), down, lines[7 + n], lines[5 + n], lines[6 + n])


def solution(mesh):
    split = P("tower", "dp", None, None)
    in_specs = (split, P("tower", "dp")) + (P(),) * 14
    out_specs = (P(), split) + (P(),) * 13
    body = partial(local, mesh.shape["dp"], mesh.shape["tower"])
    return jax.shard_map(body, mesh=mesh, in_specs=in_specs, out_specs=out_specs, check_vma=False)
```

time: 808 us -> 513 us (0.63)
  Pallas kernels: 0 us -> 241 us
  waiting for transfers between devices: 376 us -> 201 us
  matrix products: 169 us -> 0 us
  local copies, waits for them, and re-layouts: 99.7 us -> 18.2 us
  blocking collectives: 81.1 us -> 0 us
  other arithmetic: 54.3 us -> 5.45 us
  starting transfers between devices: 0.04 us -> 36.8 us
  between operations: 16.7 us -> 1.47 us
    psum x1 -> x0, waiting for transfers between devices: 376 us -> none  [local(): lax.psum((grad_w_qkv, grad_q_bias, grad_v_bias, grad_w_out, grad_out_bias...]
    pallas_call x0 -> x32, Pallas kernels: none -> 241 us  [the longest x19 112 us: call(): return made if dep is None else lambda *args: made(*args, dep)]
    ppermute x0 -> x44, waiting for transfers between devices: none -> 201 us  [the longest x39 192 us: move(): return lax.ppermute(value, ('dp', 'tower'), pairs)]
    dot_general x29 -> x0, matrix products: 169 us -> none  [the longest x1 35.1 us: local(): jnp.dot(hidden_low, w_up, preferred_element_type=jnp.float32) + up_bias]
    psum x1 -> x0, blocking collectives: 43.5 us -> none  [local(): lax.psum((grad_w_qkv, grad_q_bias, grad_v_bias, grad_w_out, grad_out_bias...]
    all_gather x2 -> x0, blocking collectives: 37.6 us -> none  [the longest x1 31.4 us: local(): everything = lax.all_gather(grouped, 'dp', axis=1, tiled=True)]
    ppermute x0 -> x44, starting transfers between devices: none -> 36.8 us  [the longest x39 26.9 us: move(): return lax.ppermute(value, ('dp', 'tower'), pairs)]
    reduce_sum x15 -> x0, other arithmetic: 25.5 us -> none  [the longest x1 5.24 us: local(): proj_sums = jnp.sum(grad_proj.astype(jnp.float32), axis=0)]
  transfers between devices with their start and end apart: 1 -> 44, of which waited for: 1 -> 23; matrix products, arithmetic and copies ran while one was open for 2% -> 1% of each run, Pallas kernels for 0% -> 23%
where the time goes in v1:
time: 513 us; the launch traced here: 504 us
  Pallas kernels  241 us (47%)
  waiting for transfers between devices  201 us (39%)
  starting transfers between devices  36.8 us (7%)
  local copies, waits for them, and re-layouts  18.2 us (4%)
  other arithmetic  5.45 us (1%)
    ppermute x39, waiting for transfers between devices, move(): return lax.ppermute(value, ('dp', 'tower'), pairs)  192 us
    pallas_call x19, Pallas kernels, call(): return made if dep is None else lambda *args: made(*args, dep)  112 us
    pallas_call x6, Pallas kernels, gather(): pl.pallas_call(run, in_specs=ins + ([] if dep is None else [ANY]), out_sp...  32.9 us
    pallas_call x1, Pallas kernels, feed(): pl.pallas_call(partial(feed_body, tile, span, 768), grid=(rows // tile,),...  29.1 us
    ppermute x39, starting transfers between devices, move(): return lax.ppermute(value, ('dp', 'tower'), pairs)  26.9 us
    pallas_call x2, Pallas kernels, attend_back(): pl.pallas_call(partial(attend_back_body, seq, span, group), grid=(width /...  24.3 us
    pallas_call x1, Pallas kernels, attend(): pl.pallas_call(partial(attend_body, seqs, span, group), grid=(steps,), in...  20.7 us
    unnamed x56, local copies, waits for them, and re-layouts  10.7 us
  transfers between devices with their start and end apart: 44, of which 23 were waited for; matrix products, arithmetic and copies ran while one was open for 1% of the time, Pallas kernels for 23%

profile of v1, /device:TPU:0, one launch (start us, length us, event | category | flops | bytes accessed | tf_op | source)
XLA Modules:
  0.0 503.8 jit_solution(4572749433555958101)
XLA Ops:
  1.3 20.7 %attend.1 = (bf16[1024,768]{1,0:T(8,128)(2,1)}, bf16[1024,768]{1,0:T(8,128)(2,1)}, bf16[1024,768]{1,0:T(8,128)(2,1)}, bf16[1024,768]{1,0:T(8,128)(2,1)}, f32[3,2,4,512]{3,2,1,0:T(4,128)}) custom-call(s32[1,2]{1,0:T(1,128)} %counts.9, bf16[1024,768]{1,0:T(8,128)(2,1)} %bitcast.27, bf16[768,2304]{1,0:T(8,128)(2,1)} %wv.3, bf16[768,2304]{1,0:T(8,128)(2,1)} %wv.3, ...), custom_call_target="tpu_custom_call" | custom-call | flops 1 | bytes 1 | tf_op jit(solution)/shard_map/attend/pallas_call | solution.py:104
  22.1 29.1 %feed.1 = (bf16[768,1024]{1,0:T(8,128)(2,1)}, f32[1024,768]{1,0:T(8,128)}, f32[1024,1]{1,0:T(8,128)}, bf16[1024,3072]{1,0:T(8,128)(2,1)}, f32[1024,3072]{1,0:T(8...) custom-call(s32[1,2]{1,0:T(1,128)} %counts.9, bf16[1024,768]{1,0:T(8,128)(2,1)} %bitcast.28, ...), custom_call_target="tpu_custom_call" | custom-call | flops 1 | bytes 1 | tf_op jit(solution)/shard_map/feed/pallas_call | solution.py:171
  51.9 4.0 collective-permute-start
  67.2 2.2 collective-permute-done.3
  70.9 2.5 concatenate.26.every
  73.4 6.6 %loss.1 = (f32[1,1]{1,0:T(1,128)}, f32[1024,768]{1,0:T(8,128)}, bf16[1024,768]{1,0:T(8,128)(2,1)}, f32[8,768]{1,0:T(8,128)}) custom-call(s32[1,2]{1,0:T(1,128)} %counts.9, s32[1,1]{1,0:T(1,128)} %bitcast.own, s32[32]{0:T(128)} %pos.1, f32[64,768]{1,0:T(8,128)} %concatenate.26.every, f32[2,768]{1,0:T(2,128)} %get-tuple-element.70.sums, f32[768]{0:T(1024)} %g2.1, ...), custom_call_target="tpu_custom_call" | custom-call | flops 1 | bytes 1 | tf_op jit(solution)/shard_map/loss/pallas_call | solution.py:256
  80.0 6.8 %down_send.1.refs_3_ = f32[1536,768]{1,0:T(8,128)} custom-call(s32[1]{0:T(128)} %bitcast.4.refs_0_, bf16[1024,3072]{1,0:T(8,128)(2,1)} %get-tuple-element.76.refs_1_.refs_2_, bf16[1024,768]{1,0:T(8,128)(2,1)} %get-tuple-element.74.refs_2_.refs_0_.refs_3_), custom_call_target="tpu_custom_call" | custom-call | flops 1 | bytes 1 | tf_op jit(solution)/shard_map/down_send/pallas_call | solution.py:347
  87.5 13.1 %slope_back.1 = (bf16[1024,3072]{1,0:T(8,128)(2,1)}, f32[1,3072]{1,0:T(1,128)}) custom-call(bf16[1024,768]{1,0:T(8,128)(2,1)} %get-tuple-element.74.refs_2_.refs_0_.refs_3_, f32[1024,3072]{1,0:T(8,128)} %get-tuple-element.75.refs_1_, bf16[3072,768]{1,0:T(8,128)(2,1)} %refs_2_.1, f32[1536,768]{1,0:T(8,128)} %down_send.1.refs_3_), custom_call_target="tpu_custom_call" | custom-call | flops 1 | bytes 1 | tf_op jit(solution)/shard_map/slope_back/pallas_call | solution.py:44
  100.6 8.8 %down_keep.1 = (f32[768,768]{1,0:T(8,128)}, f32[768,768]{1,0:T(8,128)}) custom-call(s32[1]{0:T(128)} %bitcast.5.refs_0_, s32[4]{0:T(128)} %pad_add_fusion.refs_1_, bf16[1024,3072]{1,0:T(8,128)(2,1)} %get-tuple-element.76.refs_1_.refs_2_, bf16[1024,768]{1,0:T(8,128)(2,1)} %get-tuple-element.74.refs_2_.refs_0_.refs_3_, ...), custom_call_target="tpu_custom_call" | custom-call | flops 1 | bytes 1 | tf_op jit(solution)/shard_map/down_keep/pallas_call | solution.py:44
  109.5 7.8 %up_send.1.refs_7_ = f32[384,3072]{1,0:T(8,128)} custom-call(s32[1]{0:T(128)} %bitcast.4.refs_0_, bf16[768,1024]{1,0:T(8,128)(2,1)} %get-tuple-element.81.refs_1_.refs_2_.refs_3_.refs_4_.refs_5_, bf16[768,1024]{1,0:T(8,128)(2,1)} %get-tuple-element.81.refs_1_.refs_2_.refs_3_.refs_4_.refs_5_, ...), custom_call_target="tpu_custom_call" | custom-call | flops 1 | bytes 1 | tf_op jit(solution)/shard_map/up_send/pallas_call | solution.py:44
  120.2 16.4 %middle_back.1 = (f32[1024,768]{1,0:T(8,128)}, bf16[1024,768]{1,0:T(8,128)(2,1)}, bf16[1024,768]{1,0:T(8,128)(2,1)}, f32[8,768]{1,0:T(8,128)}) custom-call(bf16[1024,3072]{1,0:T(8,128)(2,1)} %get-tuple-element.77.refs_5_.refs_0_.refs_6_, bf16[768,3072]{1,0:T(8,128)(2,1)} %refs_1_.1, f32[1024,768]{1,0:T(8,128)} %get-tuple-element.78.refs_2_, ...), custom_call_target="tpu_custom_call" | custom-call | flops 1 | bytes 1 | tf_op jit(solution)/shard_map/middle_back/pallas_call | solution.py:44
  136.6 10.3 %collective-permute-done.7.refs_2_ = f32[768,768]{1,0:T(8,128)} collective-permute-done((f32[768,768]{1,0:T(8,128)}, f32[768,768]{1,0:T(8,128)}, u32[]{:S(2)}, u32[]{:S(2)}) %collective-permute-start.7) | collective-permute-done | bytes 2359328 | tf_op jit(solution)/shard_map/ppermute | solution.py:657
  146.9 4.6 add_split.6
  151.5 10.1 %up_keep.1 = (f32[192,3072]{1,0:T(8,128)}, f32[192,3072]{1,0:T(8,128)}) custom-call(s32[1]{0:T(128)} %bitcast.5.refs_0_, s32[4]{0:T(128)} %pad_add_fusion.1.refs_1_, bf16[768,1024]{1,0:T(8,128)(2,1)} %get-tuple-element.81.refs_1_.refs_2_.refs_3_.refs_4_.refs_5_, bf16[768,1024]{1,0:T(8,128)(2,1)} %get-tuple-element.81.refs_1_.refs_2_.refs_3_.refs_4_.refs_5_, ...), custom_call_target="tpu_custom_call" | custom-call | flops 1 | bytes 1 | tf_op jit(solution)/shard_map/up_keep/pallas_call | solution.py:44
  165.0 12.1 %attend_back.2 = (bf16[512,768]{1,0:T(8,128)(2,1)}, bf16[512,768]{1,0:T(8,128)(2,1)}, bf16[512,768]{1,0:T(8,128)(2,1)}, f32[1,768]{1,0:T(1,128)}, f32[1,768]{1,0:T(1,128)}) custom-call(s32[1,2]{1,0:T(1,128)} %counts.9, bf16[1024,768]{1,0:T(8,128)(2,1)} %get-tuple-element.90.q, bf16[1024,768]{1,0:T(8,128)(2,1)} %get-tuple-element.91.k, ...), custom_call_target="tpu_custom_call" | custom-call | flops 1 | bytes 1 | tf_op jit(solution)/shard_map/attend_back/pallas_call | solution.py:494
  177.0 15.5 %collective-permute-done.9.refs_2_ = f32[384,768]{1,0:T(8,128)S(1)} collective-permute-done((f32[384,768]{1,0:T(8,128)}, f32[384,768]{1,0:T(8,128)S(1)}, u32[]{:S(2)}, u32[]{:S(2)}) %collective-permute-start.9) | collective-permute-done | bytes 1179680 | tf_op jit(solution)/shard_map/ppermute | solution.py:657
  193.6 2.8 add_split.7
  199.2 12.2 %attend_back.3 = (bf16[512,768]{1,0:T(8,128)(2,1)}, bf16[512,768]{1,0:T(8,128)(2,1)}, bf16[512,768]{1,0:T(8,128)(2,1)}, f32[1,768]{1,0:T(1,128)}, f32[1,768]{1,0:T(1,128)}) custom-call(s32[1,2]{1,0:T(1,128)} %counts.9, bf16[1024,768]{1,0:T(8,128)(2,1)} %get-tuple-element.90.q, bf16[1024,768]{1,0:T(8,128)(2,1)} %get-tuple-element.91.k, ...), custom_call_target="tpu_custom_call" | custom-call | flops 1 | bytes 1 | tf_op jit(solution)/shard_map/attend_back/pallas_call | solution.py:494
  214.4 2.2 add.145.refs_3_.refs_0_
  216.6 4.6 add_split.8
  221.2 8.2 %last_send.1.refs_3_ = f32[1600,768]{1,0:T(8,128)} custom-call(s32[1]{0:T(128)} %bitcast.4.refs_0_, bf16[1024,768]{1,0:T(8,128)(2,1)} %bitcast.29, bf16[1024,768]{1,0:T(8,128)(2,1)} %get-tuple-element.69.ctx.refs_2_.refs_3_, bf16[1024,768]{1,0:T(8,128)(2,1)} %get-tuple-element.85.refs_3_.refs_4_, f32[16,768]{1,0:T(8,128)} %pad.4.refs_4_.refs_5_, ...), custom_call_target="tpu_custom_call" | custom-call | flops 1 | bytes 1 | tf_op jit(solution)/shard_map/last_send/pallas_call | solution.py:44
  230.9 2.6 collective-permute-start.13
  233.5 12.3 %collective-permute-done.11.refs_2_ = f32[96,3072]{1,0:T(8,128)S(1)} collective-permute-done((f32[96,3072]{1,0:T(8,128)}, f32[96,3072]{1,0:T(8,128)S(1)}, u32[]{:S(2)}, u32[]{:S(2)}) %collective-permute-start.11) | collective-permute-done | bytes 1179680 | tf_op jit(solution)/shard_map/ppermute | solution.py:657
  246.8 2.7 add_split.9
  249.5 8.9 %token_grad.1.refs_2_ = f32[1024,768]{1,0:T(8,128)} custom-call(f32[1024,768]{1,0:T(8,128)} %get-tuple-element.83.dres1, bf16[768,2304]{1,0:T(8,128)(2,1)} %wv.3, bf16[768,2304]{1,0:T(8,128)(2,1)} %wv.3, bf16[768,2304]{1,0:T(8,128)(2,1)} %wv.3, f32[48,3072]{1,0:T(8,128)} %get-tuple-element.112.dep.refs_0_, ...), custom_call_target="tpu_custom_call" | custom-call | flops 1 | bytes 1 | tf_op jit(solution)/shard_map/token_grad/pallas_call | solution.py:524
  258.8 2.1 add.146.refs_13_.refs_1_
  261.0 12.1 %last_keep.1 = (f32[800,768]{1,0:T(8,128)}, f32[800,768]{1,0:T(8,128)}) custom-call(s32[1]{0:T(128)} %bitcast.5.refs_0_, s32[4]{0:T(128)} %pad_add_fusion.1.refs_1_, bf16[1024,768]{1,0:T(8,128)(2,1)} %bitcast.30, bf16[1024,768]{1,0:T(8,128)(2,1)} %get-tuple-element.69.ctx.refs_2_.refs_3_, bf16[1024,768]{1,0:T(8,128)(2,1)} %get-tuple-element.85.refs_3_.refs_4_, ...), custom_call_target="tpu_custom_call" | custom-call | flops 1 | bytes 1 | tf_op jit(solution)/shard_map/last_keep/pallas_call | solution.py:44
  276.7 14.4 %collective-permute-done.15.refs_1_ = f32[48,3072]{1,0:T(8,128)S(1)} collective-permute-done((f32[48,3072]{1,0:T(8,128)}, f32[48,3072]{1,0:T(8,128)S(1)}, u32[]{:S(2)}, u32[]{:S(2)}) %collective-permute-start.15) | collective-permute-done | bytes 589856 | tf_op jit(solution)/shard_map/ppermute | solution.py:657
  295.8 15.1 %collective-permute-done.17.refs_2_ = f32[192,768]{1,0:T(8,128)S(1)} collective-permute-done((f32[192,768]{1,0:T(8,128)S(1)}, f32[192,768]{1,0:T(8,128)S(1)}, u32[]{:S(2)}, u32[]{:S(2)}) %collective-permute-start.17) | collective-permute-done | bytes 589856 | tf_op jit(solution)/shard_map/ppermute | solution.py:657
  311.7 2.9 gather.6.refs_2_.refs_1_
  315.7 5.1 %collective-permute-done.16.refs_1_ = f32[48,3072]{1,0:T(8,128)S(1)} collective-permute-done((f32[48,3072]{1,0:T(8,128)}, f32[48,3072]{1,0:T(8,128)S(1)}, u32[]{:S(2)}, u32[]{:S(2)}) %collective-permute-start.16) | collective-permute-done | bytes 589856 | tf_op jit(solution)/shard_map/ppermute | solution.py:657
  323.7 5.1 %add_split.10 = (f32[400,768]{1,0:T(8,128)}, f32[400,768]{1,0:T(8,128)}) custom-call(s32[1]{0:T(128)} %bitcast.11.refs_0_, f32[800,768]{1,0:T(8,128)} %get-tuple-element.113.refs_2_.refs_1_, f32[800,768]{1,0:T(8,128)} %collective-permute-done.14.refs_2_, f32[48,3072]{1,0:T(8,128)} %add.148.refs_3_.refs_1_), custom_call_target="tpu_custom_call" | custom-call | flops 1 | bytes 1 | tf_op jit(solution)/shard_map/add_split/pallas_call | solution.py:44
  331.5 11.5 %collective-permute-done.19.refs_2_ = f32[48,3072]{1,0:T(8,128)S(1)} collective-permute-done((f32[48,3072]{1,0:T(8,128)S(1)}, f32[48,3072]{1,0:T(8,128)S(1)}, u32[]{:S(2)}, u32[]{:S(2)}) %collective-permute-start.19) | collective-permute-done | bytes 589856 | tf_op jit(solution)/shard_map/ppermute | solution.py:657
  343.9 2.8 gather.7.refs_3_.refs_1_
  346.8 12.3 %collective-permute-done.18.refs_2_ = f32[400,768]{1,0:T(8,128)} collective-permute-done((f32[400,768]{1,0:T(8,128)}, f32[400,768]{1,0:T(8,128)}, u32[]{:S(2)}, u32[]{:S(2)}) %collective-permute-start.18) | collective-permute-done | bytes 1228832 | tf_op jit(solution)/shard_map/ppermute | solution.py:657
  359.1 2.8 add_split.11
  362.4 18.0 %collective-permute-done.24.refs_4_ = f32[384,768]{1,0:T(8,128)} collective-permute-done((f32[384,768]{1,0:T(8,128)}, f32[384,768]{1,0:T(8,128)}, u32[]{:S(2)}, u32[]{:S(2)}) %collective-permute-start.24) | collective-permute-done | bytes 1179680 | tf_op jit(solution)/shard_map/ppermute | solution.py:657
  384.2 2.1 add.149.refs_9_.refs_0_
  388.4 10.3 %collective-permute-done.31.refs_3_ = f32[96,3072]{1,0:T(8,128)} collective-permute-done((f32[96,3072]{1,0:T(8,128)}, f32[96,3072]{1,0:T(8,128)}, u32[]{:S(2)}, u32[]{:S(2)}) %collective-permute-start.31) | collective-permute-done | bytes 1179680 | tf_op jit(solution)/shard_map/ppermute | solution.py:657
  398.7 12.6 %collective-permute-done.32.refs_4_ = f32[96,3072]{1,0:T(8,128)} collective-permute-done((f32[96,3072]{1,0:T(8,128)}, f32[96,3072]{1,0:T(8,128)}, u32[]{:S(2)}, u32[]{:S(2)}) %collective-permute-start.32) | collective-permute-done | bytes 1179680 | tf_op jit(solution)/shard_map/ppermute | solution.py:657
  412.0 8.1 %gather.8.refs_2_ = f32[3072,768]{1,0:T(8,128)} custom-call(s32[8]{0:T(128)} %stack.106.refs_0_, f32[384,768]{1,0:T(8,128)} %gather.6.refs_2_.refs_1_, f32[384,768]{1,0:T(8,128)} %collective-permute-done.22.refs_2_, f32[384,768]{1,0:T(8,128)} %collective-permute-done.23.refs_3_, f32[384,768]{1,0:T(8,128)} %collective-permute-done.24.refs_4_, ...), custom_call_target="tpu_custom_call" | custom-call | flops 1 | bytes 1 | tf_op jit(solution)/shard_map/gather/pallas_call | solution.py:631
  420.9 2.2 add.150.refs_9_.refs_1_
  423.5 8.1 %gather.9.refs_3_ = f32[768,3072]{1,0:T(8,128)} custom-call(s32[8]{0:T(128)} %stack.106.refs_0_, f32[96,3072]{1,0:T(8,128)} %gather.7.refs_3_.refs_1_, f32[96,3072]{1,0:T(8,128)} %collective-permute-done.30.refs_2_, f32[96,3072]{1,0:T(8,128)} %collective-permute-done.31.refs_3_, f32[96,3072]{1,0:T(8,128)} %collective-permute-done.32.refs_4_, ...), custom_call_target="tpu_custom_call" | custom-call | flops 1 | bytes 1 | tf_op jit(solution)/shard_map/gather/pallas_call | solution.py:631
  431.6 7.9 %collective-permute-done.29.refs_2_ = f32[200,768]{1,0:T(8,128)S(1)} collective-permute-done((f32[200,768]{1,0:T(8,128)}, f32[200,768]{1,0:T(8,128)S(1)}, u32[]{:S(2)}, u32[]{:S(2)}) %collective-permute-start.29) | collective-permute-done | bytes 614432 | tf_op jit(solution)/shard_map/ppermute | solution.py:657
  440.4 2.9 gather.10.refs_1_.refs_9_
  444.4 27.9 %collective-permute-done.37.refs_2_ = f32[400,768]{1,0:T(8,128)S(1)} collective-permute-done((f32[400,768]{1,0:T(8,128)}, f32[400,768]{1,0:T(8,128)S(1)}, u32[]{:S(2)}, u32[]{:S(2)}) %collective-permute-start.37) | collective-permute-done | bytes 1228832 | tf_op jit(solution)/shard_map/ppermute | solution.py:657
  473.7 15.2 %collective-permute-done.39.refs_4_ = f32[400,768]{1,0:T(8,128)S(1)} collective-permute-done((f32[400,768]{1,0:T(8,128)S(1)}, f32[400,768]{1,0:T(8,128)S(1)}, u32[]{:S(2)}, u32[]{:S(2)}) %collective-permute-start.39) | collective-permute-done | bytes 1228832 | tf_op jit(solution)/shard_map/ppermute | solution.py:657
  492.0 8.3 %gather.11 = (f32[768,2304]{1,0:T(8,128)}, f32[768,768]{1,0:T(8,128)}, f32[16,768]{1,0:T(8,128)}) custom-call(s32[8]{0:T(128)} %stack.106.refs_0_, f32[400,768]{1,0:T(8,128)} %gather.10.refs_1_.refs_9_, f32[400,768]{1,0:T(8,128)} %copy-done.5, f32[400,768]{1,0:T(8,128)} %copy-done.6, f32[400,768]{1,0:T(8,128)} %copy-done.7, f32[400,768]{1,0:T(8,128)} %copy-done.8, ...), custom_call_target="tpu_custom_call" | custom-call | flops 1 | bytes 1 | tf_op jit(solution)/shard_map/gather/pallas_call | solution.py:631
  (151 shorter events, 65.3 us)
Async XLA Ops:
  22.0 29.1 %copy-start.21 = (f32[768]{0:T(1024)S(1)}, f32[768]{0:T(1024)}, u32[]{:S(2)}) copy-start(f32[768]{0:T(1024)} %g2.1) | copy-start | bytes 9220
  22.0 29.1 %copy-start.25 = (f32[768]{0:T(1024)S(1)}, f32[768]{0:T(1024)}, u32[]{:S(2)}) copy-start(f32[768]{0:T(1024)} %param.31) | copy-start | bytes 9220
  51.9 5.7 %collective-permute-start = (f32[2,768]{1,0:T(2,128)S(1)}, f32[2,768]{1,0:T(2,128)S(1)}, u32[]{:S(2)}, u32[]{:S(2)}) collective-permute-start(f32[2,768]{1,0:T(2,128)S(1)} %divide_add_fusion), channel_id=1, source_target_pairs={{0,16},{1,17},{2,18},{3,19},{4,20},{5,21},{6,22},{7,23},{8,24},{9,... | collective-permute-start | bytes 18440 | tf_op jit(solution)/shard_map/ppermute | solution.py:682
  57.6 3.8 collective-permute-start.1
  61.4 3.9 collective-permute-start.2
  65.3 4.2 collective-permute-start.3
  69.5 1.4 collective-permute-start.4
  86.8 13.8 %collective-permute-start.5 = (f32[1536,768]{1,0:T(8,128)}, f32[1536,768]{1,0:T(8,128)}, u32[]{:S(2)}, u32[]{:S(2)}) collective-permute-start(f32[1536,768]{1,0:T(8,128)} %down_send.1.refs_3_), channel_id=1, source_target_pairs={{0,1},{1,0},{2,3},{3,2},{4,5},{5,4},{6,7},{7,6},{8,9},{9,8},{10,11... | collective-permute-start | bytes 14155784 | tf_op jit(solution)/shard_map/ppermute | solution.py:657
  117.3 34.2 %collective-permute-start.6 = (f32[384,3072]{1,0:T(8,128)}, f32[384,3072]{1,0:T(8,128)}, u32[]{:S(2)}, u32[]{:S(2)}) collective-permute-start(f32[384,3072]{1,0:T(8,128)} %up_send.1.refs_7_), channel_id=1, source_target_pairs={{0,1},{1,0},{2,3},{3,2},{4,5},{5,4},{6,7},{7,6},{8,9},{9,8},{10,11... | collective-permute-start | bytes 14155784 | tf_op jit(solution)/shard_map/ppermute | solution.py:657
  117.7 29.2 %collective-permute-start.7 = (f32[768,768]{1,0:T(8,128)}, f32[768,768]{1,0:T(8,128)}, u32[]{:S(2)}, u32[]{:S(2)}) collective-permute-start(f32[768,768]{1,0:T(8,128)} %get-tuple-element.84), channel_id=1, source_target_pairs={{0,4},{1,3},{2,6},{3,1},{4,0},{5,7},{6,2},{7,5},{8,12},{9,11},{10,... | collective-permute-start | bytes 7077896 | tf_op jit(solution)/shard_map/ppermute | solution.py:657
  161.6 55.0 %collective-permute-start.8 = (f32[192,3072]{1,0:T(8,128)}, f32[192,3072]{1,0:T(8,128)}, u32[]{:S(2)}, u32[]{:S(2)}) collective-permute-start(f32[192,3072]{1,0:T(8,128)} %get-tuple-element.88), channel_id=1, source_target_pairs={{0,4},{1,3},{2,6},{3,1},{4,0},{5,7},{6,2},{7,5},{8,12},{9,11},{10,... | collective-permute-start | bytes 7077896 | tf_op jit(solution)/shard_map/ppermute | solution.py:657
  163.5 29.1 %collective-permute-start.9 = (f32[384,768]{1,0:T(8,128)}, f32[384,768]{1,0:T(8,128)S(1)}, u32[]{:S(2)}, u32[]{:S(2)}) collective-permute-start(f32[384,768]{1,0:T(8,128)} %get-tuple-element.89), channel_id=1, source_target_pairs={{0,2},{1,5},{2,0},{3,7},{4,6},{5,1},{6,4},{7,3},{8,10},{9,13},{10,... | collective-permute-start | bytes 3538952 | tf_op jit(solution)/shard_map/ppermute | solution.py:657
  196.4 17.3 %collective-permute-start.10 = (f32[192,768]{1,0:T(8,128)}, f32[192,768]{1,0:T(8,128)S(1)}, u32[]{:S(2)}, u32[]{:S(2)}) collective-permute-start(f32[192,768]{1,0:T(8,128)} %get-tuple-element.97), channel_id=1, source_target_pairs={{0,8},{1,9},{2,10},{3,11},{4,12},{5,13},{6,14},{7,15},{8,0},{9,1},... | collective-permute-start | bytes 1769480 | tf_op jit(solution)/shard_map/ppermute | solution.py:657
  229.4 31.6 %collective-permute-start.12 = (f32[1600,768]{1,0:T(8,128)}, f32[1600,768]{1,0:T(8,128)}, u32[]{:S(2)}, u32[]{:S(2)}) collective-permute-start(f32[1600,768]{1,0:T(8,128)} %last_send.1.refs_3_), channel_id=1, source_target_pairs={{0,1},{1,0},{2,3},{3,2},{4,5},{5,4},{6,7},{7,6},{8,9},{9,8},{10,11... | collective-permute-start | bytes 14745608 | tf_op jit(solution)/shard_map/ppermute | solution.py:657
  229.4 16.4 %collective-permute-start.11 = (f32[96,3072]{1,0:T(8,128)}, f32[96,3072]{1,0:T(8,128)S(1)}, u32[]{:S(2)}, u32[]{:S(2)}) collective-permute-start(f32[96,3072]{1,0:T(8,128)} %get-tuple-element.100), channel_id=1, source_target_pairs={{0,2},{1,5},{2,0},{3,7},{4,6},{5,1},{6,4},{7,3},{8,10},{9,13},{10,... | collective-permute-start | bytes 3538952 | tf_op jit(solution)/shard_map/ppermute | solution.py:657
  230.9 27.9 %collective-permute-start.13 = (f32[192,768]{1,0:T(8,128)S(1)}, f32[192,768]{1,0:T(8,128)}, u32[]{:S(2)}, u32[]{:S(2)}) collective-permute-start(f32[192,768]{1,0:T(8,128)S(1)} %copy-done.3), channel_id=1, source_target_pairs={{0,16},{1,17},{2,18},{3,19},{4,20},{5,21},{6,22},{7,23},{8,24},{9,... | collective-permute-start | bytes 1769480 | tf_op jit(solution)/shard_map/ppermute | solution.py:657
  273.1 50.6 %collective-permute-start.14 = (f32[800,768]{1,0:T(8,128)}, f32[800,768]{1,0:T(8,128)}, u32[]{:S(2)}, u32[]{:S(2)}) collective-permute-start(f32[800,768]{1,0:T(8,128)} %get-tuple-element.114), channel_id=1, source_target_pairs={{0,4},{1,3},{2,6},{3,1},{4,0},{5,7},{6,2},{7,5},{8,12},{9,11},{10,... | collective-permute-start | bytes 7372808 | tf_op jit(solution)/shard_map/ppermute | solution.py:657
  274.7 16.5 %collective-permute-start.15 = (f32[48,3072]{1,0:T(8,128)}, f32[48,3072]{1,0:T(8,128)S(1)}, u32[]{:S(2)}, u32[]{:S(2)}) collective-permute-start(f32[48,3072]{1,0:T(8,128)} %get-tuple-element.115), channel_id=1, source_target_pairs={{0,8},{1,9},{2,10},{3,11},{4,12},{5,13},{6,14},{7,15},{8,0},{9,1},... | collective-permute-start | bytes 1769480 | tf_op jit(solution)/shard_map/ppermute | solution.py:657
  274.7 36.2 %collective-permute-start.17 = (f32[192,768]{1,0:T(8,128)S(1)}, f32[192,768]{1,0:T(8,128)S(1)}, u32[]{:S(2)}, u32[]{:S(2)}) collective-permute-start(f32[192,768]{1,0:T(8,128)S(1)} %copy-done.2), channel_id=1, source_target_pairs={{0,8},{1,9},{2,10},{3,11},{4,12},{5,13},{6,14},{7,15},{8,0},{9,1},... | collective-permute-start | bytes 1769480 | tf_op jit(solution)/shard_map/ppermute | solution.py:657
  294.1 26.7 %collective-permute-start.16 = (f32[48,3072]{1,0:T(8,128)}, f32[48,3072]{1,0:T(8,128)S(1)}, u32[]{:S(2)}, u32[]{:S(2)}) collective-permute-start(f32[48,3072]{1,0:T(8,128)} %add.147.refs_3_.refs_0_), channel_id=1, source_target_pairs={{0,16},{1,17},{2,18},{3,19},{4,20},{5,21},{6,22},{7,23},{8,24},{9,... | collective-permute-start | bytes 1769480 | tf_op jit(solution)/shard_map/ppermute | solution.py:657
  314.5 17.0 %collective-permute-start.22 = (f32[384,768]{1,0:T(8,128)}, f32[384,768]{1,0:T(8,128)}, u32[]{:S(2)}, u32[]{:S(2)}) collective-permute-start(f32[384,768]{1,0:T(8,128)} %gather.6.refs_2_.refs_1_), channel_id=1, source_target_pairs={{0,2},{1,5},{2,0},{3,7},{4,6},{5,1},{6,4},{7,3},{8,10},{9,13},{10,... | collective-permute-start | bytes 3538952 | tf_op jit(solution)/shard_map/ppermute | solution.py:657
  328.8 30.3 %collective-permute-start.18 = (f32[400,768]{1,0:T(8,128)}, f32[400,768]{1,0:T(8,128)}, u32[]{:S(2)}, u32[]{:S(2)}) collective-permute-start(f32[400,768]{1,0:T(8,128)} %get-tuple-element.117), channel_id=1, source_target_pairs={{0,2},{1,5},{2,0},{3,7},{4,6},{5,1},{6,4},{7,3},{8,10},{9,13},{10,... | collective-permute-start | bytes 3686408 | tf_op jit(solution)/shard_map/ppermute | solution.py:657
  328.8 14.3 %collective-permute-start.19 = (f32[48,3072]{1,0:T(8,128)S(1)}, f32[48,3072]{1,0:T(8,128)S(1)}, u32[]{:S(2)}, u32[]{:S(2)}) collective-permute-start(f32[48,3072]{1,0:T(8,128)S(1)} %copy-done.4), channel_id=1, source_target_pairs={{0,8},{1,9},{2,10},{3,11},{4,12},{5,13},{6,14},{7,15},{8,0},{9,1},... | collective-permute-start | bytes 1769480 | tf_op jit(solution)/shard_map/ppermute | solution.py:657
  328.9 32.9 %collective-permute-start.23 = (f32[384,768]{1,0:T(8,128)S(1)}, f32[384,768]{1,0:T(8,128)}, u32[]{:S(2)}, u32[]{:S(2)}) collective-permute-start(f32[384,768]{1,0:T(8,128)S(1)} %copy-done), channel_id=1, source_target_pairs={{0,4},{1,3},{2,6},{3,1},{4,0},{5,7},{6,2},{7,5},{8,12},{9,11},{10,... | collective-permute-start | bytes 3538952 | tf_op jit(solution)/shard_map/ppermute | solution.py:657
  330.8 31.1 %collective-permute-start.25 = (f32[384,768]{1,0:T(8,128)S(1)}, f32[384,768]{1,0:T(8,128)}, u32[]{:S(2)}, u32[]{:S(2)}) collective-permute-start(f32[384,768]{1,0:T(8,128)S(1)} %copy-done), channel_id=1, source_target_pairs={{0,1},{1,0},{2,3},{3,2},{4,5},{5,4},{6,7},{7,6},{8,9},{9,8},{10,11... | collective-permute-start | bytes 3538952 | tf_op jit(solution)/shard_map/ppermute | solution.py:657
  331.5 48.8 %collective-permute-start.24 = (f32[384,768]{1,0:T(8,128)}, f32[384,768]{1,0:T(8,128)}, u32[]{:S(2)}, u32[]{:S(2)}) collective-permute-start(f32[384,768]{1,0:T(8,128)} %collective-permute-done.22.refs_2_), channel_id=1, source_target_pairs={{0,4},{1,3},{2,6},{3,1},{4,0},{5,7},{6,2},{7,5},{8,12},{9,11},{10,... | collective-permute-start | bytes 3538952 | tf_op jit(solution)/shard_map/ppermute | solution.py:657
  346.7 35.5 %collective-permute-start.30 = (f32[96,3072]{1,0:T(8,128)}, f32[96,3072]{1,0:T(8,128)}, u32[]{:S(2)}, u32[]{:S(2)}) collective-permute-start(f32[96,3072]{1,0:T(8,128)} %gather.7.refs_3_.refs_1_), channel_id=1, source_target_pairs={{0,2},{1,5},{2,0},{3,7},{4,6},{5,1},{6,4},{7,3},{8,10},{9,13},{10,... | collective-permute-start | bytes 3538952 | tf_op jit(solution)/shard_map/ppermute | solution.py:657
  361.8 20.5 %collective-permute-start.20 = (f32[200,768]{1,0:T(8,128)}, f32[200,768]{1,0:T(8,128)S(1)}, u32[]{:S(2)}, u32[]{:S(2)}) collective-permute-start(f32[200,768]{1,0:T(8,128)} %get-tuple-element.119), channel_id=1, source_target_pairs={{0,8},{1,9},{2,10},{3,11},{4,12},{5,13},{6,14},{7,15},{8,0},{9,1},... | collective-permute-start | bytes 1843208 | tf_op jit(solution)/shard_map/ppermute | solution.py:657
  361.8 24.5 %collective-permute-start.27 = (f32[384,768]{1,0:T(8,128)}, f32[384,768]{1,0:T(8,128)}, u32[]{:S(2)}, u32[]{:S(2)}) collective-permute-start(f32[384,768]{1,0:T(8,128)} %collective-permute-done.23.refs_3_), channel_id=1, source_target_pairs={{0,1},{1,0},{2,3},{3,2},{4,5},{5,4},{6,7},{7,6},{8,9},{9,8},{10,11... | collective-permute-start | bytes 3538952 | tf_op jit(solution)/shard_map/ppermute | solution.py:657
  361.9 25.9 %copy-start.1 = (f32[96,3072]{1,0:T(8,128)S(1)}, f32[96,3072]{1,0:T(8,128)}, u32[]{:S(2)}) copy-start(f32[96,3072]{1,0:T(8,128)} %gather.7.refs_3_.refs_1_) | copy-start | bytes 3538948
  361.9 25.9 %collective-permute-start.26 = (f32[384,768]{1,0:T(8,128)}, f32[384,768]{1,0:T(8,128)}, u32[]{:S(2)}, u32[]{:S(2)}) collective-permute-start(f32[384,768]{1,0:T(8,128)} %collective-permute-done.22.refs_2_), channel_id=1, source_target_pairs={{0,1},{1,0},{2,3},{3,2},{4,5},{5,4},{6,7},{7,6},{8,9},{9,8},{10,11... | collective-permute-start | bytes 3538952 | tf_op jit(solution)/shard_map/ppermute | solution.py:657
  380.4 7.5 %collective-permute-start.28 = (f32[384,768]{1,0:T(8,128)}, f32[384,768]{1,0:T(8,128)}, u32[]{:S(2)}, u32[]{:S(2)}) collective-permute-start(f32[384,768]{1,0:T(8,128)} %collective-permute-done.24.refs_4_), channel_id=1, source_target_pairs={{0,1},{1,0},{2,3},{3,2},{4,5},{5,4},{6,7},{7,6},{8,9},{9,8},{10,11... | collective-permute-start | bytes 3538952 | tf_op jit(solution)/shard_map/ppermute | solution.py:657
  382.2 16.5 %collective-permute-start.31 = (f32[96,3072]{1,0:T(8,128)}, f32[96,3072]{1,0:T(8,128)}, u32[]{:S(2)}, u32[]{:S(2)}) collective-permute-start(f32[96,3072]{1,0:T(8,128)} %gather.7.refs_3_.refs_1_), channel_id=1, source_target_pairs={{0,4},{1,3},{2,6},{3,1},{4,0},{5,7},{6,2},{7,5},{8,12},{9,11},{10,... | collective-permute-start | bytes 3538952 | tf_op jit(solution)/shard_map/ppermute | solution.py:657
  382.3 29.1 %collective-permute-start.32 = (f32[96,3072]{1,0:T(8,128)}, f32[96,3072]{1,0:T(8,128)}, u32[]{:S(2)}, u32[]{:S(2)}) collective-permute-start(f32[96,3072]{1,0:T(8,128)} %collective-permute-done.30.refs_2_), channel_id=1, source_target_pairs={{0,4},{1,3},{2,6},{3,1},{4,0},{5,7},{6,2},{7,5},{8,12},{9,11},{10,... | collective-permute-start | bytes 3538952 | tf_op jit(solution)/shard_map/ppermute | solution.py:657
  386.4 33.7 %collective-permute-start.21 = (f32[200,768]{1,0:T(8,128)}, f32[200,768]{1,0:T(8,128)S(1)}, u32[]{:S(2)}, u32[]{:S(2)}) collective-permute-start(f32[200,768]{1,0:T(8,128)} %add.149.refs_9_.refs_0_), channel_id=1, source_target_pairs={{0,16},{1,17},{2,18},{3,19},{4,20},{5,21},{6,22},{7,23},{8,24},{9,... | collective-permute-start | bytes 1843208 | tf_op jit(solution)/shard_map/ppermute | solution.py:657
  387.9 35.7 %collective-permute-start.33 = (f32[96,3072]{1,0:T(8,128)S(1)}, f32[96,3072]{1,0:T(8,128)}, u32[]{:S(2)}, u32[]{:S(2)}) collective-permute-start(f32[96,3072]{1,0:T(8,128)S(1)} %copy-done.1), channel_id=1, source_target_pairs={{0,1},{1,0},{2,3},{3,2},{4,5},{5,4},{6,7},{7,6},{8,9},{9,8},{10,11... | collective-permute-start | bytes 3538952 | tf_op jit(solution)/shard_map/ppermute | solution.py:657
  387.9 35.6 %collective-permute-start.34 = (f32[96,3072]{1,0:T(8,128)}, f32[96,3072]{1,0:T(8,128)}, u32[]{:S(2)}, u32[]{:S(2)}) collective-permute-start(f32[96,3072]{1,0:T(8,128)} %collective-permute-done.30.refs_2_), channel_id=1, source_target_pairs={{0,1},{1,0},{2,3},{3,2},{4,5},{5,4},{6,7},{7,6},{8,9},{9,8},{10,11... | collective-permute-start | bytes 3538952 | tf_op jit(solution)/shard_map/ppermute | solution.py:657
  398.7 24.8 %collective-permute-start.35 = (f32[96,3072]{1,0:T(8,128)}, f32[96,3072]{1,0:T(8,128)}, u32[]{:S(2)}, u32[]{:S(2)}) collective-permute-start(f32[96,3072]{1,0:T(8,128)} %collective-permute-done.31.refs_3_), channel_id=1, source_target_pairs={{0,1},{1,0},{2,3},{3,2},{4,5},{5,4},{6,7},{7,6},{8,9},{9,8},{10,11... | collective-permute-start | bytes 3538952 | tf_op jit(solution)/shard_map/ppermute | solution.py:657
  411.4 12.2 %collective-permute-start.36 = (f32[96,3072]{1,0:T(8,128)}, f32[96,3072]{1,0:T(8,128)}, u32[]{:S(2)}, u32[]{:S(2)}) collective-permute-start(f32[96,3072]{1,0:T(8,128)} %collective-permute-done.32.refs_4_), channel_id=1, source_target_pairs={{0,1},{1,0},{2,3},{3,2},{4,5},{5,4},{6,7},{7,6},{8,9},{9,8},{10,11... | collective-permute-start | bytes 3538952 | tf_op jit(solution)/shard_map/ppermute | solution.py:657
  423.1 16.5 %collective-permute-start.29 = (f32[200,768]{1,0:T(8,128)}, f32[200,768]{1,0:T(8,128)S(1)}, u32[]{:S(2)}, u32[]{:S(2)}) collective-permute-start(f32[200,768]{1,0:T(8,128)} %add.150.refs_9_.refs_1_), channel_id=1, source_target_pairs={{0,8},{1,9},{2,10},{3,11},{4,12},{5,13},{6,14},{7,15},{8,0},{9,1},... | collective-permute-start | bytes 1843208 | tf_op jit(solution)/shard_map/ppermute | solution.py:657
  443.2 29.0 %collective-permute-start.37 = (f32[400,768]{1,0:T(8,128)}, f32[400,768]{1,0:T(8,128)S(1)}, u32[]{:S(2)}, u32[]{:S(2)}) collective-permute-start(f32[400,768]{1,0:T(8,128)} %gather.10.refs_1_.refs_9_), channel_id=1, source_target_pairs={{0,2},{1,5},{2,0},{3,7},{4,6},{5,1},{6,4},{7,3},{8,10},{9,13},{10,... | collective-permute-start | bytes 3686408 | tf_op jit(solution)/shard_map/ppermute | solution.py:657
  444.3 29.3 %collective-permute-start.38 = (f32[400,768]{1,0:T(8,128)}, f32[400,768]{1,0:T(8,128)S(1)}, u32[]{:S(2)}, u32[]{:S(2)}) collective-permute-start(f32[400,768]{1,0:T(8,128)} %gather.10.refs_1_.refs_9_), channel_id=1, source_target_pairs={{0,4},{1,3},{2,6},{3,1},{4,0},{5,7},{6,2},{7,5},{8,12},{9,11},{10,... | collective-permute-start | bytes 3686408 | tf_op jit(solution)/shard_map/ppermute | solution.py:657
  472.2 19.8 %copy-start.5 = (f32[400,768]{1,0:T(8,128)}, f32[400,768]{1,0:T(8,128)S(1)}, u32[]{:S(2)}) copy-start(f32[400,768]{1,0:T(8,128)S(1)} %collective-permute-done.37.refs_2_) | copy-start | bytes 3686404
  472.2 16.7 %collective-permute-start.39 = (f32[400,768]{1,0:T(8,128)S(1)}, f32[400,768]{1,0:T(8,128)S(1)}, u32[]{:S(2)}, u32[]{:S(2)}) collective-permute-start(f32[400,768]{1,0:T(8,128)S(1)} %collective-permute-done.37.refs_2_), channel_id=1, source_target_pairs={{0,4},{1,3},{2,6},{3,1},{4,0},{5,7},{6,2},{7,5},{8,12},{9,11},{10,... | collective-permute-start | bytes 3686408 | tf_op jit(solution)/shard_map/ppermute | solution.py:657
  473.1 15.8 %collective-permute-start.40 = (f32[400,768]{1,0:T(8,128)}, f32[400,768]{1,0:T(8,128)S(1)}, u32[]{:S(2)}, u32[]{:S(2)}) collective-permute-start(f32[400,768]{1,0:T(8,128)} %gather.10.refs_1_.refs_9_), channel_id=1, source_target_pairs={{0,1},{1,0},{2,3},{3,2},{4,5},{5,4},{6,7},{7,6},{8,9},{9,8},{10,11... | collective-permute-start | bytes 3686408 | tf_op jit(solution)/shard_map/ppermute | solution.py:657
  473.1 15.9 %collective-permute-start.41 = (f32[400,768]{1,0:T(8,128)S(1)}, f32[400,768]{1,0:T(8,128)S(1)}, u32[]{:S(2)}, u32[]{:S(2)}) collective-permute-start(f32[400,768]{1,0:T(8,128)S(1)} %collective-permute-done.37.refs_2_), channel_id=1, source_target_pairs={{0,1},{1,0},{2,3},{3,2},{4,5},{5,4},{6,7},{7,6},{8,9},{9,8},{10,11... | collective-permute-start | bytes 3686408 | tf_op jit(solution)/shard_map/ppermute | solution.py:657
  473.6 15.3 %collective-permute-start.42 = (f32[400,768]{1,0:T(8,128)S(1)}, f32[400,768]{1,0:T(8,128)S(1)}, u32[]{:S(2)}, u32[]{:S(2)}) collective-permute-start(f32[400,768]{1,0:T(8,128)S(1)} %collective-permute-done.38.refs_3_), channel_id=1, source_target_pairs={{0,1},{1,0},{2,3},{3,2},{4,5},{5,4},{6,7},{7,6},{8,9},{9,8},{10,11... | collective-permute-start | bytes 3686408 | tf_op jit(solution)/shard_map/ppermute | solution.py:657
  489.0 3.0 collective-permute-start.43
  (24 other events, 104.2 us)
